TPU v7x, 256 devices: a whole 4x4x8 slice. The times are simulated.
256 devices in a mesh: heads: 16 (over y_hi, x, core), seq: 16 (over z, y_lo).
Axes of the slice: x: 4, y: 4 (y_hi: 2, y_lo: 2; y = y_hi * 2 + y_lo), z: 8, core: 2. Of those that a mesh axis runs over, the one named last changes fastest.
Arguments:
- queries: bfloat16 [4096, 2048], P('seq', 'heads'), may hold values from -250 to 250
- key_rows: bfloat16 [4096, 256], P('seq'), may hold values from -4 to 4
- value_rows: bfloat16 [4096, 256], P('seq'), may hold values from -4 to 4
- layer_grad: bfloat16 [4096, 8192], P('seq', 'heads'), may hold values from -6 to 6
- w_out: bfloat16 [2048, 8192], P(None, 'heads'), may hold values from -0.09375 to 0.09375
- block_order: int32 [32], replicated, may hold values from 0 to 31, each once
- doc_lengths: int32 [4], replicated, may hold values from 1 to 2048, 4096 in all
Outputs:
- query_grad: bfloat16 [4096, 2048], P('seq', 'heads')
- key_grad: bfloat16 [4096, 256], P('seq')
- value_grad: bfloat16 [4096, 256], P('seq')
- head_grad: bfloat16 [4096, 2048], P('seq', 'heads')
Inputs may be any that keep to these rules, and one draw needn't show every extreme that they name: `block_order`: a permutation of the (32) sequence blocks. `doc_lengths`: the documents' lengths sum to 4096; the longest holds half of 4096.
All inputs are finite; a program needn't handle non-finite values.
Results may differ from a plain program's by a relative error of at most 0.03.
Values may be sent and summed in bfloat16 or wider, within the bound.
A program may use at most 64 MiB of HBM per device.

v0:
```python
import math

import jax
import jax.numpy as jnp
from jax import lax
from jax.sharding import PartitionSpec as P

GROUP = 8


neg_large = -1e30


def shifted(array, axis, by):
    size = lax.axis_size(axis)
    return lax.ppermute(array, axis, [(i, (i + by) % size) for i in range(size)])


def contract_last(left, right):
    return lax.dot_general(
        left, right, (((1,), (1,)), ((), ())), preferred_element_type=jnp.float32
    )


def contract_first(left, right):
    return lax.dot_general(
        left, right, (((0,), (0,)), ((), ())), preferred_element_type=jnp.float32
    )


def slot_rows(block_order, slot_index, block_rows):
    leading = lax.dynamic_slice_in_dim(block_order, slot_index, 1)[0]
    return leading * block_rows + jnp.arange(block_rows, dtype=jnp.int32)


def doc_begin(positions, doc_lengths):
    starts = jnp.cumsum(doc_lengths) - doc_lengths
    inside = starts[None, :] <= positions[:, None]
    return jnp.max(jnp.where(inside, starts[None, :], 0), axis=1)


def block_part(array, which, block_rows):
    return array[which * block_rows : (which + 1) * block_rows]


def allowed_pairs(query_pos, query_begin, key_pos):
    return (key_pos[None, :] <= query_pos[:, None]) & (key_pos[None, :] >= query_begin[:, None])


def forward_tile(running, query_block, key_block, score_scale):
    allowed = allowed_pairs(query_block[1], query_block[2], key_block[2])

    def forward_update(current):
        row_top, row_sum, weighted = current
        scores = jnp.where(
            allowed, contract_last(query_block[0], key_block[0]) * score_scale, neg_large
        )
        new_top = jnp.maximum(row_top, jnp.max(scores, axis=1))
        weights = jnp.where(allowed, jnp.exp(scores - new_top[:, None]), 0.0)
        factor = jnp.exp(row_top - new_top)
        row_sum = row_sum * factor + jnp.sum(weights, axis=1)
        weighted = weighted * factor[:, None] + jnp.dot(
            weights, key_block[1].astype(jnp.float32), precision=lax.Precision.HIGHEST
        )
        return (new_top, row_sum, weighted)

    return lax.cond(jnp.any(allowed), forward_update, lambda current: current, running)


def forward_visit(running, query_blocks, key_blocks, score_scale):
    running = list(running)
    for query_slot in range(len(query_blocks)):
        for key_slot in range(len(key_blocks)):
            running[query_slot] = forward_tile(
                running[query_slot], query_blocks[query_slot], key_blocks[key_slot], score_scale
            )
    return tuple(running)


def backward_tile(partial_value, query_block, key_block, score_scale):
    allowed = allowed_pairs(query_block[4], query_block[5], key_block[2])

    def backward_update(current):
        query_part, key_part, value_part = current
        scores = jnp.where(
            allowed, contract_last(query_block[0], key_block[0]) * score_scale, neg_large
        )
        probabilities = jnp.where(allowed, jnp.exp(scores - query_block[2][:, None]), 0.0)
        value_part = value_part + contract_first(probabilities.astype(jnp.bfloat16), query_block[1])
        dprobs = contract_last(query_block[1], key_block[1])
        dscores = (probabilities * (dprobs - query_block[3][:, None])).astype(jnp.bfloat16)
        query_part = query_part + jnp.dot(dscores, key_block[0], preferred_element_type=jnp.float32)
        key_part = key_part + contract_first(dscores, query_block[0])
        return (query_part, key_part, value_part)

    return lax.cond(jnp.any(allowed), backward_update, lambda current: current, partial_value)


def backward_visit(query_grads, key_grads, query_blocks, key_blocks, score_scale):
    query_grads = list(query_grads)
    key_grads = list(key_grads)
    for query_slot in range(len(query_blocks)):
        for key_slot in range(len(key_blocks)):
            result = backward_tile(
                (query_grads[query_slot], key_grads[key_slot][0], key_grads[key_slot][1]),
                query_blocks[query_slot],
                key_blocks[key_slot],
                score_scale,
            )
            query_grads[query_slot] = result[0]
            key_grads[key_slot] = (result[1], result[2])
    return (tuple(query_grads), tuple(key_grads))


def local(queries, key_rows, value_rows, layer_grad, w_out, block_order, doc_lengths):
    block_rows = queries.shape[0] // 2
    head_size = queries.shape[1]
    cycle_size = lax.axis_size("seq")
    seq_index = lax.axis_index("seq")
    shared_head = lax.axis_index("heads") // GROUP
    score_scale = 1.0 / math.sqrt(head_size)
    head_grad = (
        lax.psum_scatter(
            contract_last(w_out, layer_grad).astype(jnp.bfloat16),
            "heads",
            scatter_dimension=0,
            tiled=True,
        )
        .astype(jnp.float32)
        .T.astype(jnp.bfloat16)
    )
    own_keys = lax.dynamic_slice_in_dim(key_rows, shared_head * head_size, head_size, 1)
    own_values = lax.dynamic_slice_in_dim(value_rows, shared_head * head_size, head_size, 1)
    local_pos = jnp.concatenate(
        [
            slot_rows(block_order, 2 * seq_index, block_rows),
            slot_rows(block_order, 2 * seq_index + 1, block_rows),
        ]
    )
    local_begin = doc_begin(local_pos, doc_lengths)
    forward_queries = tuple(
        (
            (
                block_part(queries, which, block_rows),
                block_part(local_pos, which, block_rows),
                block_part(local_begin, which, block_rows),
            )
            for which in range(2)
        )
    )
    local_keys = tuple(
        (
            (
                block_part(own_keys, which, block_rows),
                block_part(own_values, which, block_rows),
                block_part(local_pos, which, block_rows),
            )
            for which in range(2)
        )
    )
    running = tuple(
        (
            (
                jnp.full((block_rows,), neg_large, jnp.float32),
                jnp.zeros((block_rows,), jnp.float32),
                jnp.zeros((block_rows, head_size), jnp.float32),
            )
            for which in range(2)
        )
    )
    running = forward_visit(running, forward_queries, local_keys, score_scale)

    def forward_hop(rotation, loop_state):
        running, pieces = loop_state
        pieces = shifted((pieces[0], pieces[1], pieces[2], pieces[3]), "seq", 1)
        source = (seq_index - rotation) % cycle_size
        visiting = (
            (pieces[0], pieces[1], slot_rows(block_order, 2 * source, block_rows)),
            (pieces[2], pieces[3], slot_rows(block_order, 2 * source + 1, block_rows)),
        )
        return (forward_visit(running, forward_queries, visiting, score_scale), pieces)

    start_pieces = (local_keys[0][0], local_keys[0][1], local_keys[1][0], local_keys[1][1])
    running, _ = lax.fori_loop(1, cycle_size, forward_hop, (running, start_pieces))
    row_top = jnp.concatenate([item[0] for item in running])
    row_sum = jnp.concatenate([item[1] for item in running])
    weighted = jnp.concatenate([item[2] for item in running])
    log_norm = row_top + jnp.log(row_sum)
    attended = weighted / row_sum[:, None]
    row_dots = jnp.sum(head_grad.astype(jnp.float32) * attended, axis=1)
    empty = jnp.zeros((block_rows, head_size), jnp.float32)
    bundle = (queries, head_grad, log_norm, row_dots)

    def make_block(pieces, positions):
        return (
            pieces[0],
            pieces[1],
            pieces[2],
            pieces[3],
            positions,
            doc_begin(positions, doc_lengths),
        )

    local_blocks = tuple(
        (
            make_block(
                tuple((block_part(item, which, block_rows) for item in bundle)),
                block_part(local_pos, which, block_rows),
            )
            for which in range(2)
        )
    )
    query_grads, key_grads = backward_visit(
        (empty, empty), ((empty, empty), (empty, empty)), local_blocks, local_keys, score_scale
    )

    def backward_hop(rotation, loop_state):
        moving, key_grads = loop_state
        moving = shifted(moving, "seq", 1)
        source = (seq_index - rotation) % cycle_size
        positions = (
            slot_rows(block_order, 2 * source, block_rows),
            slot_rows(block_order, 2 * source + 1, block_rows),
        )
        query_blocks = tuple(
            (
                make_block(
                    tuple((block_part(item, which, block_rows) for item in moving[:4])),
                    positions[which],
                )
                for which in range(2)
            )
        )
        query_grads, key_grads = backward_visit(
            (block_part(moving[4], 0, block_rows), block_part(moving[4], 1, block_rows)),
            key_grads,
            query_blocks,
            local_keys,
            score_scale,
        )
        return (moving[:4] + (jnp.concatenate(query_grads),), key_grads)

    moving, key_grads = lax.fori_loop(
        1, cycle_size, backward_hop, (bundle + (jnp.concatenate(query_grads),), key_grads)
    )
    query_grad = shifted(moving[4].astype(jnp.bfloat16), "seq", 1).astype(jnp.float32)
    key_grad = jnp.concatenate([key_grads[0][0], key_grads[1][0]])
    value_grad = jnp.concatenate([key_grads[0][1], key_grads[1][1]])
    placed_zero = jnp.zeros((2 * block_rows, key_rows.shape[1]), jnp.float32)
    placed_keys = lax.dynamic_update_slice_in_dim(
        placed_zero, key_grad * score_scale, shared_head * head_size, 1
    )
    placed_values = lax.dynamic_update_slice_in_dim(
        placed_zero, value_grad, shared_head * head_size, 1
    )
    key_sum, value_sum = (
        lax.psum(placed_keys.astype(jnp.bfloat16), "heads").astype(jnp.float32),
        lax.psum(placed_values.astype(jnp.bfloat16), "heads").astype(jnp.float32),
    )
    return (
        (query_grad * score_scale).astype(jnp.bfloat16),
        key_sum.astype(jnp.bfloat16),
        value_sum.astype(jnp.bfloat16),
        head_grad,
    )


def solution(mesh):
    return jax.shard_map(
        local,
        mesh=mesh,
        in_specs=(
            P("seq", "heads"),
            P("seq", None),
            P("seq", None),
            P("seq", "heads"),
            P(None, "heads"),
            P(),
            P(),
        ),
        out_specs=(P("seq", "heads"), P("seq", None), P("seq", None), P("seq", "heads")),
        check_vma=False,
    )
```

profile of v0, /device:TPU:1, one launch (start us, length us, event | category | flops | bytes accessed | tf_op | source)
XLA Modules:
  0.0 594.0 jit_solution(13994692358103950087)
XLA Ops:
  8.8 2.7 convolution_convert_fusion
  17.7 2.9 conditional.16
  21.2 2.6 conditional.19
  23.8 190.1 %while.66 = (s32[]{:T(128)}, f32[128]{0:T(128)}, f32[128]{0:T(128)S(1)}, f32[128,128]{1,0:T(8,128)S(1)}, f32[128]{0:T(128)}, /*index=5*/f32[128]{0:T(128)S(1)}, ...) while((s32[]{:T(128)}, f32[128]{0:T(128)}, ...), condition=%wide.region_44.45_spmd.clone, body=%wide.region_23.44_spmd.clone.sunk | while | flops 118359568 | bytes 2791498 | solution.py:184
  38.0 2.5 conditional.43
  40.7 3.2 collective-permute-start.1
  75.4 3.0 collective-permute-start
  88.3 3.2 collective-permute-start
  99.3 2.5 conditional.42
  111.0 2.5 conditional.42
  121.0 2.5 conditional.43
  123.7 5.5 collective-permute-start.1
  134.8 2.5 conditional.42
  137.4 3.8 collective-permute-start
  147.3 2.5 conditional.42
  149.8 2.5 conditional.43
  160.5 5.1 collective-permute-start
  187.8 4.3 collective-permute-start
  198.3 2.5 conditional.42
  203.4 2.6 collective-permute-start.3
  211.4 2.5 conditional.43
  222.3 179.1 %while.67 = (s32[]{:T(128)}, bf16[256,128]{1,0:T(8,128)(2,1)S(1)}, bf16[256,128]{1,0:T(8,128)(2,1)S(1)}, f32[256]{0:T(256)S(1)}, f32[256]{0:T(256)S(1)}, /*index...) while((s32[]{:T(128)}, bf16[256,128]{1,0:T(8,128)(2,1)S(1)}, ...), condition=%wide.region_75.76_spmd.clone, body=%wide.region_60.75_spmd.clone.sunk | while | flops 84905240 | bytes 5927186 | solution.py:243
  222.5 4.7 collective-permute-start.5
  227.3 2.7 collective-permute-start.8
  237.0 2.5 collective-permute-start.8
  256.2 3.5 collective-permute-start.4
  259.8 4.7 collective-permute-start.6
  293.3 3.7 collective-permute-start.5
  331.0 3.3 collective-permute-start.6
  377.9 3.0 collective-permute-start.6
  402.4 4.8 collective-permute-done.9
  407.8 176.2 %all-reduce.3.cloned.1.call-done = (bf16[256,256]{1,0:T(8,128)(2,1)}, bf16[256,256]{1,0:T(8,128)(2,1)}) async-done(((bf16[256,256]{1,0:T(8,128)(2,1)}, bf16[256,256]{1,0:T(8,128)(2,1)}), (bf16[256,256]{1,0:T(8,128)(2,1)}, bf16[256,256]{1,0:T(8,128)(2,1)})) %all-reduce.3.cloned.1.call-update) | async-done | bytes 262160 | tf_op jit(solution)/shard_map/psum | solution.py:257
  (971 shorter events, 244.3 us)
Async XLA Ops:
  7.2 210.3 %reduce-scatter.2.cloned.1.call-start = ((), (), s32[]{:S(2)}) async-start(), calls=%async_computation.1 | async-start | bytes 1114112 | tf_op jit(solution)/shard_map/reduce_scatter | solution.py:123
  11.6 572.5 %all-reduce.3.cloned.1.call-start = ((), (), s32[]{:S(2)}) async-start(), calls=%async_computation.2 | async-start | bytes 524288 | tf_op jit(solution)/shard_map/psum | solution.py:257
  23.9 11.8 %collective-permute-start = (bf16[128,128]{1,0:T(8,128)(2,1)S(1)}, bf16[128,128]{1,0:T(8,128)(2,1)S(1)}, u32[]{:S(2)}, u32[]{:S(2)}) collective-permute-start(bf16[128,128]{1,0:T(8,128)(2,1)S(1)} %get-tuple-element.2402), channel_id=1, source_target_pairs={{0,1},{1,2},{2,3},{3,4},{4,5},{5,6},{6,7},{7,8},{8,9},{9,10},{10,1... | collective-permute-start | bytes 98312 | tf_op jit(solution)/shard_map/while/body/eval_jaxpr/ppermute | solution.py:16
  27.6 10.4 %collective-permute-start.2 = (bf16[128,128]{1,0:T(8,128)(2,1)S(1)}, bf16[128,128]{1,0:T(8,128)(2,1)S(1)}, u32[]{:S(2)}, u32[]{:S(2)}) collective-permute-start(bf16[128,128]{1,0:T(8,128)(2,1)S(1)} %get-tuple-element.2404), channel_id=1, source_target_pairs={{0,1},{1,2},{2,3},{3,4},{4,5},{5,6},{6,7},{7,8},{8,9},{9,10},{10,1... | collective-permute-start | bytes 98312 | tf_op jit(solution)/shard_map/while/body/eval_jaxpr/ppermute | solution.py:16
  75.4 10.5 %collective-permute-start = (bf16[128,128]{1,0:T(8,128)(2,1)S(1)}, bf16[128,128]{1,0:T(8,128)(2,1)S(1)}, u32[]{:S(2)}, u32[]{:S(2)}) collective-permute-start(bf16[128,128]{1,0:T(8,128)(2,1)S(1)} %get-tuple-element.2402), channel_id=1, source_target_pairs={{0,1},{1,2},{2,3},{3,4},{4,5},{5,6},{6,7},{7,8},{8,9},{9,10},{10,1... | collective-permute-start | bytes 98312 | tf_op jit(solution)/shard_map/while/body/eval_jaxpr/ppermute | solution.py:16
  88.3 10.9 %collective-permute-start = (bf16[128,128]{1,0:T(8,128)(2,1)S(1)}, bf16[128,128]{1,0:T(8,128)(2,1)S(1)}, u32[]{:S(2)}, u32[]{:S(2)}) collective-permute-start(bf16[128,128]{1,0:T(8,128)(2,1)S(1)} %get-tuple-element.2402), channel_id=1, source_target_pairs={{0,1},{1,2},{2,3},{3,4},{4,5},{5,6},{6,7},{7,8},{8,9},{9,10},{10,1... | collective-permute-start | bytes 98312 | tf_op jit(solution)/shard_map/while/body/eval_jaxpr/ppermute | solution.py:16
  123.6 11.1 %collective-permute-start = (bf16[128,128]{1,0:T(8,128)(2,1)S(1)}, bf16[128,128]{1,0:T(8,128)(2,1)S(1)}, u32[]{:S(2)}, u32[]{:S(2)}) collective-permute-start(bf16[128,128]{1,0:T(8,128)(2,1)S(1)} %get-tuple-element.2402), channel_id=1, source_target_pairs={{0,1},{1,2},{2,3},{3,4},{4,5},{5,6},{6,7},{7,8},{8,9},{9,10},{10,1... | collective-permute-start | bytes 98312 | tf_op jit(solution)/shard_map/while/body/eval_jaxpr/ppermute | solution.py:16
  123.7 11.0 %collective-permute-start.1 = (bf16[128,128]{1,0:T(8,128)(2,1)S(1)}, bf16[128,128]{1,0:T(8,128)(2,1)S(1)}, u32[]{:S(2)}, u32[]{:S(2)}) collective-permute-start(bf16[128,128]{1,0:T(8,128)(2,1)S(1)} %get-tuple-element.2403), channel_id=1, source_target_pairs={{0,1},{1,2},{2,3},{3,4},{4,5},{5,6},{6,7},{7,8},{8,9},{9,10},{10,1... | collective-permute-start | bytes 98312 | tf_op jit(solution)/shard_map/while/body/eval_jaxpr/ppermute | solution.py:16
  137.4 9.8 %collective-permute-start = (bf16[128,128]{1,0:T(8,128)(2,1)S(1)}, bf16[128,128]{1,0:T(8,128)(2,1)S(1)}, u32[]{:S(2)}, u32[]{:S(2)}) collective-permute-start(bf16[128,128]{1,0:T(8,128)(2,1)S(1)} %get-tuple-element.2402), channel_id=1, source_target_pairs={{0,1},{1,2},{2,3},{3,4},{4,5},{5,6},{6,7},{7,8},{8,9},{9,10},{10,1... | collective-permute-start | bytes 98312 | tf_op jit(solution)/shard_map/while/body/eval_jaxpr/ppermute | solution.py:16
  160.5 13.0 %collective-permute-start = (bf16[128,128]{1,0:T(8,128)(2,1)S(1)}, bf16[128,128]{1,0:T(8,128)(2,1)S(1)}, u32[]{:S(2)}, u32[]{:S(2)}) collective-permute-start(bf16[128,128]{1,0:T(8,128)(2,1)S(1)} %get-tuple-element.2402), channel_id=1, source_target_pairs={{0,1},{1,2},{2,3},{3,4},{4,5},{5,6},{6,7},{7,8},{8,9},{9,10},{10,1... | collective-permute-start | bytes 98312 | tf_op jit(solution)/shard_map/while/body/eval_jaxpr/ppermute | solution.py:16
  187.8 10.4 %collective-permute-start = (bf16[128,128]{1,0:T(8,128)(2,1)S(1)}, bf16[128,128]{1,0:T(8,128)(2,1)S(1)}, u32[]{:S(2)}, u32[]{:S(2)}) collective-permute-start(bf16[128,128]{1,0:T(8,128)(2,1)S(1)} %get-tuple-element.2402), channel_id=1, source_target_pairs={{0,1},{1,2},{2,3},{3,4},{4,5},{5,6},{6,7},{7,8},{8,9},{9,10},{10,1... | collective-permute-start | bytes 98312 | tf_op jit(solution)/shard_map/while/body/eval_jaxpr/ppermute | solution.py:16
  200.9 10.4 %collective-permute-start = (bf16[128,128]{1,0:T(8,128)(2,1)S(1)}, bf16[128,128]{1,0:T(8,128)(2,1)S(1)}, u32[]{:S(2)}, u32[]{:S(2)}) collective-permute-start(bf16[128,128]{1,0:T(8,128)(2,1)S(1)} %get-tuple-element.2402), channel_id=1, source_target_pairs={{0,1},{1,2},{2,3},{3,4},{4,5},{5,6},{6,7},{7,8},{8,9},{9,10},{10,1... | collective-permute-start | bytes 98312 | tf_op jit(solution)/shard_map/while/body/eval_jaxpr/ppermute | solution.py:16
  200.9 10.3 %collective-permute-start.1 = (bf16[128,128]{1,0:T(8,128)(2,1)S(1)}, bf16[128,128]{1,0:T(8,128)(2,1)S(1)}, u32[]{:S(2)}, u32[]{:S(2)}) collective-permute-start(bf16[128,128]{1,0:T(8,128)(2,1)S(1)} %get-tuple-element.2403), channel_id=1, source_target_pairs={{0,1},{1,2},{2,3},{3,4},{4,5},{5,6},{6,7},{7,8},{8,9},{9,10},{10,1... | collective-permute-start | bytes 98312 | tf_op jit(solution)/shard_map/while/body/eval_jaxpr/ppermute | solution.py:16
  222.3 13.2 %collective-permute-start.4 = (bf16[256,128]{1,0:T(8,128)(2,1)S(1)}, bf16[256,128]{1,0:T(8,128)(2,1)S(1)}, u32[]{:S(2)}, u32[]{:S(2)}) collective-permute-start(bf16[256,128]{1,0:T(8,128)(2,1)S(1)} %get-tuple-element.2501), channel_id=1, source_target_pairs={{0,1},{1,2},{2,3},{3,4},{4,5},{5,6},{6,7},{7,8},{8,9},{9,10},{10,1... | collective-permute-start | bytes 196616 | tf_op jit(solution)/shard_map/while/body/eval_jaxpr/ppermute | solution.py:16
  222.5 13.1 %collective-permute-start.5 = (bf16[256,128]{1,0:T(8,128)(2,1)S(1)}, bf16[256,128]{1,0:T(8,128)(2,1)S(1)}, u32[]{:S(2)}, u32[]{:S(2)}) collective-permute-start(bf16[256,128]{1,0:T(8,128)(2,1)S(1)} %get-tuple-element.2502), channel_id=1, source_target_pairs={{0,1},{1,2},{2,3},{3,4},{4,5},{5,6},{6,7},{7,8},{8,9},{9,10},{10,1... | collective-permute-start | bytes 196616 | tf_op jit(solution)/shard_map/while/body/eval_jaxpr/ppermute | solution.py:16
  256.2 14.8 %collective-permute-start.4 = (bf16[256,128]{1,0:T(8,128)(2,1)S(1)}, bf16[256,128]{1,0:T(8,128)(2,1)S(1)}, u32[]{:S(2)}, u32[]{:S(2)}) collective-permute-start(bf16[256,128]{1,0:T(8,128)(2,1)S(1)} %get-tuple-element.2501), channel_id=1, source_target_pairs={{0,1},{1,2},{2,3},{3,4},{4,5},{5,6},{6,7},{7,8},{8,9},{9,10},{10,1... | collective-permute-start | bytes 196616 | tf_op jit(solution)/shard_map/while/body/eval_jaxpr/ppermute | solution.py:16
  259.7 11.4 %collective-permute-start.5 = (bf16[256,128]{1,0:T(8,128)(2,1)S(1)}, bf16[256,128]{1,0:T(8,128)(2,1)S(1)}, u32[]{:S(2)}, u32[]{:S(2)}) collective-permute-start(bf16[256,128]{1,0:T(8,128)(2,1)S(1)} %get-tuple-element.2502), channel_id=1, source_target_pairs={{0,1},{1,2},{2,3},{3,4},{4,5},{5,6},{6,7},{7,8},{8,9},{9,10},{10,1... | collective-permute-start | bytes 196616 | tf_op jit(solution)/shard_map/while/body/eval_jaxpr/ppermute | solution.py:16
  259.8 11.2 %collective-permute-start.6 = (f32[256]{0:T(256)S(1)}, f32[256]{0:T(256)S(1)}, u32[]{:S(2)}, u32[]{:S(2)}) collective-permute-start(f32[256]{0:T(256)S(1)} %get-tuple-element.2503), channel_id=1, source_target_pairs={{0,1},{1,2},{2,3},{3,4},{4,5},{5,6},{6,7},{7,8},{8,9},{9,10},{10,1... | collective-permute-start | bytes 3080 | tf_op jit(solution)/shard_map/while/body/eval_jaxpr/ppermute | solution.py:16
  292.3 13.4 %collective-permute-start.4 = (bf16[256,128]{1,0:T(8,128)(2,1)S(1)}, bf16[256,128]{1,0:T(8,128)(2,1)S(1)}, u32[]{:S(2)}, u32[]{:S(2)}) collective-permute-start(bf16[256,128]{1,0:T(8,128)(2,1)S(1)} %get-tuple-element.2501), channel_id=1, source_target_pairs={{0,1},{1,2},{2,3},{3,4},{4,5},{5,6},{6,7},{7,8},{8,9},{9,10},{10,1... | collective-permute-start | bytes 196616 | tf_op jit(solution)/shard_map/while/body/eval_jaxpr/ppermute | solution.py:16
  293.3 12.4 %collective-permute-start.5 = (bf16[256,128]{1,0:T(8,128)(2,1)S(1)}, bf16[256,128]{1,0:T(8,128)(2,1)S(1)}, u32[]{:S(2)}, u32[]{:S(2)}) collective-permute-start(bf16[256,128]{1,0:T(8,128)(2,1)S(1)} %get-tuple-element.2502), channel_id=1, source_target_pairs={{0,1},{1,2},{2,3},{3,4},{4,5},{5,6},{6,7},{7,8},{8,9},{9,10},{10,1... | collective-permute-start | bytes 196616 | tf_op jit(solution)/shard_map/while/body/eval_jaxpr/ppermute | solution.py:16
  306.6 9.8 %collective-permute-start.4 = (bf16[256,128]{1,0:T(8,128)(2,1)S(1)}, bf16[256,128]{1,0:T(8,128)(2,1)S(1)}, u32[]{:S(2)}, u32[]{:S(2)}) collective-permute-start(bf16[256,128]{1,0:T(8,128)(2,1)S(1)} %get-tuple-element.2501), channel_id=1, source_target_pairs={{0,1},{1,2},{2,3},{3,4},{4,5},{5,6},{6,7},{7,8},{8,9},{9,10},{10,1... | collective-permute-start | bytes 196616 | tf_op jit(solution)/shard_map/while/body/eval_jaxpr/ppermute | solution.py:16
  319.5 9.8 %collective-permute-start.4 = (bf16[256,128]{1,0:T(8,128)(2,1)S(1)}, bf16[256,128]{1,0:T(8,128)(2,1)S(1)}, u32[]{:S(2)}, u32[]{:S(2)}) collective-permute-start(bf16[256,128]{1,0:T(8,128)(2,1)S(1)} %get-tuple-element.2501), channel_id=1, source_target_pairs={{0,1},{1,2},{2,3},{3,4},{4,5},{5,6},{6,7},{7,8},{8,9},{9,10},{10,1... | collective-permute-start | bytes 196616 | tf_op jit(solution)/shard_map/while/body/eval_jaxpr/ppermute | solution.py:16
  319.6 9.8 %collective-permute-start.5 = (bf16[256,128]{1,0:T(8,128)(2,1)S(1)}, bf16[256,128]{1,0:T(8,128)(2,1)S(1)}, u32[]{:S(2)}, u32[]{:S(2)}) collective-permute-start(bf16[256,128]{1,0:T(8,128)(2,1)S(1)} %get-tuple-element.2502), channel_id=1, source_target_pairs={{0,1},{1,2},{2,3},{3,4},{4,5},{5,6},{6,7},{7,8},{8,9},{9,10},{10,1... | collective-permute-start | bytes 196616 | tf_op jit(solution)/shard_map/while/body/eval_jaxpr/ppermute | solution.py:16
  330.7 10.4 %collective-permute-start.4 = (bf16[256,128]{1,0:T(8,128)(2,1)S(1)}, bf16[256,128]{1,0:T(8,128)(2,1)S(1)}, u32[]{:S(2)}, u32[]{:S(2)}) collective-permute-start(bf16[256,128]{1,0:T(8,128)(2,1)S(1)} %get-tuple-element.2501), channel_id=1, source_target_pairs={{0,1},{1,2},{2,3},{3,4},{4,5},{5,6},{6,7},{7,8},{8,9},{9,10},{10,1... | collective-permute-start | bytes 196616 | tf_op jit(solution)/shard_map/while/body/eval_jaxpr/ppermute | solution.py:16
  330.8 10.3 %collective-permute-start.5 = (bf16[256,128]{1,0:T(8,128)(2,1)S(1)}, bf16[256,128]{1,0:T(8,128)(2,1)S(1)}, u32[]{:S(2)}, u32[]{:S(2)}) collective-permute-start(bf16[256,128]{1,0:T(8,128)(2,1)S(1)} %get-tuple-element.2502), channel_id=1, source_target_pairs={{0,1},{1,2},{2,3},{3,4},{4,5},{5,6},{6,7},{7,8},{8,9},{9,10},{10,1... | collective-permute-start | bytes 196616 | tf_op jit(solution)/shard_map/while/body/eval_jaxpr/ppermute | solution.py:16
  331.0 10.0 %collective-permute-start.6 = (f32[256]{0:T(256)S(1)}, f32[256]{0:T(256)S(1)}, u32[]{:S(2)}, u32[]{:S(2)}) collective-permute-start(f32[256]{0:T(256)S(1)} %get-tuple-element.2503), channel_id=1, source_target_pairs={{0,1},{1,2},{2,3},{3,4},{4,5},{5,6},{6,7},{7,8},{8,9},{9,10},{10,1... | collective-permute-start | bytes 3080 | tf_op jit(solution)/shard_map/while/body/eval_jaxpr/ppermute | solution.py:16
  341.3 11.5 %collective-permute-start.4 = (bf16[256,128]{1,0:T(8,128)(2,1)S(1)}, bf16[256,128]{1,0:T(8,128)(2,1)S(1)}, u32[]{:S(2)}, u32[]{:S(2)}) collective-permute-start(bf16[256,128]{1,0:T(8,128)(2,1)S(1)} %get-tuple-element.2501), channel_id=1, source_target_pairs={{0,1},{1,2},{2,3},{3,4},{4,5},{5,6},{6,7},{7,8},{8,9},{9,10},{10,1... | collective-permute-start | bytes 196616 | tf_op jit(solution)/shard_map/while/body/eval_jaxpr/ppermute | solution.py:16
  342.3 10.5 %collective-permute-start.5 = (bf16[256,128]{1,0:T(8,128)(2,1)S(1)}, bf16[256,128]{1,0:T(8,128)(2,1)S(1)}, u32[]{:S(2)}, u32[]{:S(2)}) collective-permute-start(bf16[256,128]{1,0:T(8,128)(2,1)S(1)} %get-tuple-element.2502), channel_id=1, source_target_pairs={{0,1},{1,2},{2,3},{3,4},{4,5},{5,6},{6,7},{7,8},{8,9},{9,10},{10,1... | collective-permute-start | bytes 196616 | tf_op jit(solution)/shard_map/while/body/eval_jaxpr/ppermute | solution.py:16
  355.8 9.9 %collective-permute-start.4 = (bf16[256,128]{1,0:T(8,128)(2,1)S(1)}, bf16[256,128]{1,0:T(8,128)(2,1)S(1)}, u32[]{:S(2)}, u32[]{:S(2)}) collective-permute-start(bf16[256,128]{1,0:T(8,128)(2,1)S(1)} %get-tuple-element.2501), channel_id=1, source_target_pairs={{0,1},{1,2},{2,3},{3,4},{4,5},{5,6},{6,7},{7,8},{8,9},{9,10},{10,1... | collective-permute-start | bytes 196616 | tf_op jit(solution)/shard_map/while/body/eval_jaxpr/ppermute | solution.py:16
  376.9 12.3 %collective-permute-start.4 = (bf16[256,128]{1,0:T(8,128)(2,1)S(1)}, bf16[256,128]{1,0:T(8,128)(2,1)S(1)}, u32[]{:S(2)}, u32[]{:S(2)}) collective-permute-start(bf16[256,128]{1,0:T(8,128)(2,1)S(1)} %get-tuple-element.2501), channel_id=1, source_target_pairs={{0,1},{1,2},{2,3},{3,4},{4,5},{5,6},{6,7},{7,8},{8,9},{9,10},{10,1... | collective-permute-start | bytes 196616 | tf_op jit(solution)/shard_map/while/body/eval_jaxpr/ppermute | solution.py:16
  376.9 12.3 %collective-permute-start.5 = (bf16[256,128]{1,0:T(8,128)(2,1)S(1)}, bf16[256,128]{1,0:T(8,128)(2,1)S(1)}, u32[]{:S(2)}, u32[]{:S(2)}) collective-permute-start(bf16[256,128]{1,0:T(8,128)(2,1)S(1)} %get-tuple-element.2502), channel_id=1, source_target_pairs={{0,1},{1,2},{2,3},{3,4},{4,5},{5,6},{6,7},{7,8},{8,9},{9,10},{10,1... | collective-permute-start | bytes 196616 | tf_op jit(solution)/shard_map/while/body/eval_jaxpr/ppermute | solution.py:16
  377.9 11.2 %collective-permute-start.6 = (f32[256]{0:T(256)S(1)}, f32[256]{0:T(256)S(1)}, u32[]{:S(2)}, u32[]{:S(2)}) collective-permute-start(f32[256]{0:T(256)S(1)} %get-tuple-element.2503), channel_id=1, source_target_pairs={{0,1},{1,2},{2,3},{3,4},{4,5},{5,6},{6,7},{7,8},{8,9},{9,10},{10,1... | collective-permute-start | bytes 3080 | tf_op jit(solution)/shard_map/while/body/eval_jaxpr/ppermute | solution.py:16
  (114 other events, 811.6 us)
Sparse Core Ops, SparseCore 0:
  12.1 77.9 reduce-scatter.1
  402.5 181.4 all-reduce.2
where the time goes:
time: 596 us; the launch traced here: 594 us
  waiting for transfers between devices  188 us (32%)
  starting transfers between devices  143 us (24%)
  loops' own time  121 us (20%)
  other arithmetic  57.7 us (10%)
  local copies, waits for them, and re-layouts  39.4 us (7%)
  matrix products  24.3 us (4%)
  between operations  20.8 us (3%)
    psum x1, waiting for transfers between devices, local(): lax.psum(placed_keys.astype(jnp.bfloat16), 'heads').astype(jnp.float32)  176 us
    ppermute x136, starting transfers between devices, shifted(): lax.ppermute(array, axis, [(i, (i + by) % size) for i in range(size)])  143 us
    another operation x1, loops' own time, local(): lax.fori_loop(1, cycle_size, backward_hop, (bundle + (jnp.concatenate(que...  59.2 us
    another operation x1, loops' own time, local(): lax.fori_loop(1, cycle_size, forward_hop, (running, start_pieces))  58.5 us
    dynamic_slice x31, local copies, waits for them, and re-layouts, slot_rows(): leading = lax.dynamic_slice_in_dim(block_order, slot_index, 1)[0]  19.8 us
    reduce_or x16, other arithmetic, backward_tile(): jnp.any(allowed)  13.5 us
    reduce_or x15, other arithmetic, forward_tile(): jnp.any(allowed)  13.1 us
    add x19, other arithmetic, forward_update(): row_sum = row_sum * factor + jnp.sum(weights, axis=1)  12.7 us
  transfers between devices with their start and end apart: 138, of which 10 were waited for; matrix products, arithmetic and copies ran while one was open for 16% of the time, Pallas kernels for 0%

commit v1 on v0

v1 whole, which is shorter than its diff:
```python
import math

import jax
import jax.numpy as jnp
from jax import lax
from jax.experimental import pallas as pl
from jax.experimental.pallas import tpu as pltpu
from jax.sharding import PartitionSpec as P

GROUP = 8
DH = 128
ROWS = 256
MESH = pl.DeviceIdType.MESH
F32 = jnp.float32
BF16 = jnp.bfloat16
NEG = -1e30


def contract_last(left, right):
    return lax.dot_general(
        left, right, (((1,), (1,)), ((), ())), preferred_element_type=F32
    )


def matmul(left, right):
    return jnp.dot(left, right, preferred_element_type=F32)


def make_kernel(n_seq):
    part = ROWS // GROUP
    keys = n_seq * part
    n_heads = 2 * GROUP
    chips = n_heads // 2
    scale = 1.0 / math.sqrt(DH)
    scale2 = scale * math.log2(math.e)

    def kernel(
        q_hbm, k_hbm, v_hbm, lg_hbm, w_hbm, bo, dl,
        qg_out, kg_out, vg_out, hg_out,
        w_v, lg_v, q_all, do_all, kv_own, kv_all, kt_v, bias,
        mine, oth_tx, oth_rx, c1_tx, c1_rx,
        e_all, dp_all, st_own, st_rx, fac, ds_own, ds_rx, dsum,
        dv_acc, dk_acc, dv_tx, dk_tx, dv_rx, dk_rx, dv_fin, dk_fin,
        dq_tx, dq_rx, qg_v,
        w_sem, ld_sem, out_sem,
        q_send, q_recv, kv_send, kv_recv, oth_send, oth_recv, c1_send, c1_recv,
        do_send, do_recv, st_send, st_recv, d_send, d_recv, dq_send, dq_recv,
        dv_send, dv_recv, dk_send, dk_recv, av_send, av_recv, ak_send, ak_recv,
    ):
        h = lax.axis_index("heads")
        s = lax.axis_index("seq")
        c = h // GROUP
        j = h % GROUP
        x = j // 2
        core = h % 2
        chip = h // 2
        sib = h + 1 - 2 * core

        def to_head(src, dst, send_sem, recv_sem, target):
            return pltpu.make_async_remote_copy(
                src_ref=src, dst_ref=dst, send_sem=send_sem, recv_sem=recv_sem,
                device_id={"heads": target}, device_id_type=MESH,
            )

        def to_seq(src, dst, send_sem, recv_sem, target):
            return pltpu.make_async_remote_copy(
                src_ref=src, dst_ref=dst, send_sem=send_sem, recv_sem=recv_sem,
                device_id={"seq": target}, device_id_type=MESH,
            )

        def await_bytes(ref, sem):
            pltpu.make_async_copy(ref, ref, sem).wait()

        row0 = pl.multiple_of(j * part, part)
        col0 = pl.multiple_of(c * DH, DH)
        lg_load = pltpu.make_async_copy(lg_hbm, lg_v, ld_sem.at[0])
        q_load = pltpu.make_async_copy(q_hbm, q_all.at[j], ld_sem.at[1])
        k_load = pltpu.make_async_copy(
            k_hbm.at[pl.ds(row0, part), pl.ds(col0, DH)],
            kv_own.at[:, pl.ds(0, DH)], ld_sem.at[2],
        )
        v_load = pltpu.make_async_copy(
            v_hbm.at[pl.ds(row0, part), pl.ds(col0, DH)],
            kv_own.at[:, pl.ds(DH, DH)], ld_sem.at[3],
        )
        q_load.start()
        k_load.start()
        v_load.start()
        lg_load.start()

        def w_load(step, which):
            target = ((chip + step + 1) % chips) * 2
            head = target + core if which == 0 else target + 1 - core
            return pltpu.make_async_copy(
                w_hbm.at[pl.ds(pl.multiple_of(head * DH, DH), DH), :],
                w_v.at[step, pl.ds(which * DH, DH), :],
                w_sem.at[step, which],
            )

        for step in range(chips):
            for which in range(2):
                w_load(step, which).start()

        barrier = pltpu.get_barrier_semaphore()
        for r in range(1, n_heads):
            pl.semaphore_signal(
                barrier, inc=1, device_id={"heads": (h + r) % n_heads}, device_id_type=MESH
            )
        for r in range(1, n_seq):
            pl.semaphore_signal(
                barrier, inc=1, device_id={"seq": (s + r) % n_seq}, device_id_type=MESH
            )

        lane = lax.broadcasted_iota(jnp.int32, (1, ROWS), 1)
        q_pos = jnp.where(
            lane < ROWS // 2,
            bo[2 * s] * (ROWS // 2) + lane,
            bo[2 * s + 1] * (ROWS // 2) + lane - ROWS // 2,
        )
        start1 = dl[0]
        start2 = start1 + dl[1]
        start3 = start2 + dl[2]
        q_begin = jnp.zeros((1, ROWS), jnp.int32)
        for begin in (start1, start2, start3):
            q_begin = jnp.maximum(q_begin, jnp.where(begin <= q_pos, begin, 0))

        def bias_step(r, carry):
            slot = (s - r + n_seq) % n_seq
            base = bo[2 * slot + j // 4] * (ROWS // 2) + (j % 4) * part
            k_pos = base + lax.broadcasted_iota(jnp.int32, (part, ROWS), 0)
            allowed = (k_pos <= q_pos) & (k_pos >= q_begin)
            bias[pl.ds(pl.multiple_of(r * part, part), part), :] = jnp.where(allowed, 0.0, NEG)
            return carry

        lax.fori_loop(0, n_seq, bias_step, 0)
        q_load.wait()
        k_load.wait()
        v_load.wait()
        pl.semaphore_wait(barrier, n_heads + n_seq - 2)

        def peer(t, q):
            return ((x - t + 4) % 4) * 2 + (core + q) % 2

        def gather_first(buf, send, recv):
            for t in (2, 1, 3):
                to_head(
                    buf.at[j], buf.at[j], send.at[2 * t], recv.at[2 * t],
                    c * GROUP + ((x + t) % 4) * 2 + core,
                ).start()
            to_head(buf.at[j], buf.at[j], send.at[1], recv.at[1], sib).start()

        def gather_wait(buf, recv, t, q):
            ref = buf.at[peer(t, q)]
            pltpu.make_async_copy(ref, ref, recv.at[2 * t + q]).wait()

        def gather_pass(buf, send, recv, t):
            gather_wait(buf, recv, t, 0)
            other = peer(t, 0)
            to_head(
                buf.at[other], buf.at[other], send.at[2 * t + 1], recv.at[2 * t + 1], sib
            ).start()

        gather_first(q_all, q_send, q_recv)

        def kv_step(r, carry):
            to_seq(
                kv_own, kv_all.at[pl.ds(pl.multiple_of(r * part, part), part), :],
                kv_send, kv_recv, (s + r) % n_seq,
            ).start()
            return carry

        lax.fori_loop(1, n_seq, kv_step, 0)
        kv_all[pl.ds(0, part), :] = kv_own[...]

        lg_load.wait()

        def c1_copy(i):
            target = ((chip + i + 1) % chips) * 2 + core
            return to_head(c1_tx.at[i], c1_rx.at[i], c1_send.at[i], c1_recv, target)

        def product_step(i, carry):
            @pl.when(i < chips)
            def _():
                for which in range(2):
                    pltpu.make_async_copy(
                        w_v.at[i, pl.ds(which * DH, DH), :],
                        w_v.at[i, pl.ds(which * DH, DH), :],
                        w_sem.at[i, which],
                    ).wait()
                product = contract_last(lg_v[...], w_v[i])
                oth_tx[i] = product[:, DH:].astype(BF16)
                to_head(oth_tx.at[i], oth_rx.at[i], oth_send.at[i], oth_recv.at[i], sib).start()
                mine[i] = product[:, :DH]

            @pl.when(i >= 2)
            def _():
                k = i - 2
                pltpu.make_async_copy(oth_rx.at[k], oth_rx.at[k], oth_recv.at[k]).wait()
                total = mine[k] + oth_rx[k].astype(F32)

                @pl.when(k < chips - 1)
                def _():
                    c1_tx[k] = total.astype(BF16)
                    c1_copy(k).start()

                @pl.when(k == chips - 1)
                def _():
                    mine[k] = total

            return carry

        lax.fori_loop(0, chips + 2, product_step, 0)

        for t in (1, 3, 2):
            gather_pass(q_all, q_send, q_recv, t)

        await_bytes(kv_all.at[pl.ds(part, keys - part), :], kv_recv)
        kt_v[...] = kv_all[:, :DH].astype(F32).T.astype(BF16)

        def score_head(head):
            sc = contract_last(kv_all[:, :DH], q_all[head]) * scale2 + bias[...]
            top = jnp.max(sc, axis=0, keepdims=True)
            e = jnp.exp2(sc - top)
            e_all[head] = e
            st_own[0, pl.ds(head, 1), :] = top
            st_own[1, pl.ds(head, 1), :] = jnp.sum(e, axis=0, keepdims=True)

        order = ((0, 0), (0, 1), (1, 0), (3, 0), (2, 0), (1, 1), (3, 1), (2, 1))
        for t, q in order:
            if q == 1:
                gather_wait(q_all, q_recv, t, q)
            score_head(peer(t, q))

        for r in range(1, GROUP):
            to_head(
                st_own, st_rx.at[r - 1], st_send, st_recv, c * GROUP + (j + r) % GROUP
            ).start()

        await_bytes(c1_rx, c1_recv)
        total = mine[chips - 1]
        for i in range(chips - 1):
            total = total + c1_rx[i].astype(F32)
        do_all[j] = total.astype(BF16)
        gather_first(do_all, do_send, do_recv)
        hg_copy = pltpu.make_async_copy(do_all.at[j], hg_out, out_sem.at[0])
        hg_copy.start()

        await_bytes(st_rx, st_recv)
        top = st_own[0]
        for r in range(GROUP - 1):
            top = jnp.maximum(top, st_rx[r, 0])
        norm = st_own[1] * jnp.exp2(st_own[0] - top)
        for r in range(GROUP - 1):
            norm = norm + st_rx[r, 1] * jnp.exp2(st_rx[r, 0] - top)
        fac[...] = jnp.exp2(st_own[0] - top) / norm

        dv_acc[...] = jnp.zeros_like(dv_acc)

        def value_head(head):
            p = e_all[head] * fac[pl.ds(head, 1), :]
            e_all[head] = p
            dp = contract_last(kv_all[:, DH:], do_all[head])
            dp_all[head] = dp
            ds_own[pl.ds(head, 1), :] = jnp.sum(p * dp, axis=0, keepdims=True)
            dv_acc[...] += matmul(p.astype(BF16), do_all[head])

        for t, q in order:
            if t > 0 and q == 0:
                gather_pass(do_all, do_send, do_recv, t)
            elif q == 1:
                gather_wait(do_all, do_recv, t, q)
            value_head(peer(t, q))

        for r in range(1, GROUP):
            to_head(
                ds_own, ds_rx.at[r - 1], d_send, d_recv, c * GROUP + (j + r) % GROUP
            ).start()

        dv_tx[...] = dv_acc[...].astype(BF16)

        def scatter(tx, rx, send, recv):
            def step(r, carry):
                rows = pl.ds(pl.multiple_of(r * part, part), part)
                to_seq(
                    tx.at[rows, :], rx.at[rows, :], send, recv, (s - r + n_seq) % n_seq
                ).start()
                return carry

            lax.fori_loop(1, n_seq, step, 0)

        scatter(dv_tx, dv_rx, dv_send, dv_recv)

        await_bytes(ds_rx, d_recv)
        total_d = ds_own[...]
        for r in range(GROUP - 1):
            total_d = total_d + ds_rx[r]
        dsum[...] = total_d

        dk_acc[...] = jnp.zeros_like(dk_acc)

        def grad_head(head):
            ds = (e_all[head] * (dp_all[head] - dsum[pl.ds(head, 1), :])).astype(BF16)
            dq_tx[head] = (matmul(kt_v[...], ds) * scale).astype(BF16)
            dk_acc[...] += matmul(ds, q_all[head])

        def dq_copy(t, q):
            head = peer(t, q)
            slot = 2 * t + q - 1
            return to_head(
                dq_tx.at[head], dq_rx.at[slot], dq_send.at[slot], dq_recv, c * GROUP + head
            )

        for t, q in ((2, 0), (2, 1), (1, 0), (1, 1), (3, 0), (3, 1), (0, 1), (0, 0)):
            grad_head(peer(t, q))
            if (t, q) != (0, 0):
                dq_copy(t, q).start()

        dk_tx[...] = (dk_acc[...] * scale).astype(BF16)
        scatter(dk_tx, dk_rx, dk_send, dk_recv)

        def finish(tx, rx, fin, out, recv, all_send, all_recv, own_sem):
            await_bytes(rx.at[pl.ds(part, keys - part), :], recv)
            summed = tx[pl.ds(0, part), :].astype(F32)
            for r in range(1, n_seq):
                summed = summed + rx[pl.ds(r * part, part), :].astype(F32)
            fin[...] = summed.astype(BF16)
            place = out.at[pl.ds(row0, part), pl.ds(col0, DH)]

            def step(r, carry):
                to_head(fin, place, all_send, all_recv, (h + r) % n_heads).start()
                return carry

            lax.fori_loop(1, n_heads, step, 0)
            pltpu.make_async_copy(fin, place, own_sem).start()

        finish(dv_tx, dv_rx, dv_fin, vg_out, dv_recv, av_send, av_recv, out_sem.at[1])
        finish(dk_tx, dk_rx, dk_fin, kg_out, dk_recv, ak_send, ak_recv, out_sem.at[2])

        await_bytes(dq_rx, dq_recv)
        query_sum = dq_tx[j].astype(F32)
        for r in range(GROUP - 1):
            query_sum = query_sum + dq_rx[r].astype(F32)
        qg_v[...] = query_sum.T.astype(BF16)
        qg_copy = pltpu.make_async_copy(qg_v, qg_out, out_sem.at[3])
        qg_copy.start()

        for slot in range(1, 2 * 4):
            await_bytes(q_all.at[0], q_send.at[slot])
            await_bytes(do_all.at[0], do_send.at[slot])
        await_bytes(kv_all.at[pl.ds(part, keys - part), :], kv_send)
        for i in range(chips):
            await_bytes(oth_tx.at[i], oth_send.at[i])
        for i in range(chips - 1):
            await_bytes(c1_tx.at[i], c1_send.at[i])
        await_bytes(st_rx, st_send)
        await_bytes(ds_rx, d_send)
        for slot in range(GROUP - 1):
            await_bytes(dq_tx.at[0], dq_send.at[slot])
        for tx, send in ((dv_tx, dv_send), (dk_tx, dk_send)):
            await_bytes(tx.at[pl.ds(part, keys - part), :], send)
        spread = (n_heads - 1) * part
        for sem in (av_send, ak_send, av_recv, ak_recv):
            await_bytes(q_all.at[pl.ds(0, 5), pl.ds(0, spread // 5), :], sem)
        hg_copy.wait()
        qg_copy.wait()
        for out, fin, index in ((vg_out, dv_fin, 1), (kg_out, dk_fin, 2)):
            place = out.at[pl.ds(row0, part), pl.ds(col0, DH)]
            pltpu.make_async_copy(fin, place, out_sem.at[index]).wait()

    return kernel


def local(queries, key_rows, value_rows, layer_grad, w_out, block_order, doc_lengths):
    n_seq = lax.axis_size("seq")
    part = ROWS // GROUP
    keys = n_seq * part
    depth = layer_grad.shape[1]
    chips = GROUP
    vmem = pltpu.VMEM
    dma = pltpu.SemaphoreType.DMA
    scratch = [
        vmem((chips, 2 * DH, depth), BF16),
        vmem((ROWS, depth), BF16),
        vmem((GROUP, ROWS, DH), BF16),
        vmem((GROUP, ROWS, DH), BF16),
        vmem((part, 2 * DH), BF16),
        vmem((keys, 2 * DH), BF16),
        vmem((DH, keys), BF16),
        vmem((keys, ROWS), F32),
        vmem((chips, ROWS, DH), F32),
        vmem((chips, ROWS, DH), BF16),
        vmem((chips, ROWS, DH), BF16),
        vmem((chips - 1, ROWS, DH), BF16),
        vmem((chips - 1, ROWS, DH), BF16),
        vmem((GROUP, keys, ROWS), F32),
        vmem((GROUP, keys, ROWS), F32),
        vmem((2, GROUP, ROWS), F32),
        vmem((GROUP - 1, 2, GROUP, ROWS), F32),
        vmem((GROUP, ROWS), F32),
        vmem((GROUP, ROWS), F32),
        vmem((GROUP - 1, GROUP, ROWS), F32),
        vmem((GROUP, ROWS), F32),
        vmem((keys, DH), F32),
        vmem((keys, DH), F32),
        vmem((keys, DH), BF16),
        vmem((keys, DH), BF16),
        vmem((keys, DH), BF16),
        vmem((keys, DH), BF16),
        vmem((part, DH), BF16),
        vmem((part, DH), BF16),
        vmem((GROUP, DH, ROWS), BF16),
        vmem((GROUP - 1, DH, ROWS), BF16),
        vmem((ROWS, DH), BF16),
        dma((chips, 2)),
        dma((4,)),
        dma((4,)),
        dma((8,)),
        dma((8,)),
        dma,
        dma,
        dma((chips,)),
        dma((chips,)),
        dma((chips - 1,)),
        dma,
        dma((8,)),
        dma((8,)),
        dma,
        dma,
        dma,
        dma,
        dma((GROUP - 1,)),
        dma,
        dma,
        dma,
        dma,
        dma,
        dma,
        dma,
        dma,
        dma,
    ]
    anywhere = pl.BlockSpec(memory_space=pl.ANY)
    scalars = pl.BlockSpec(memory_space=pltpu.SMEM)
    return pl.pallas_call(
        make_kernel(n_seq),
        out_shape=(
            jax.ShapeDtypeStruct(queries.shape, BF16),
            jax.ShapeDtypeStruct(key_rows.shape, BF16),
            jax.ShapeDtypeStruct(value_rows.shape, BF16),
            jax.ShapeDtypeStruct(queries.shape, BF16),
        ),
        in_specs=[anywhere] * 5 + [scalars] * 2,
        out_specs=(anywhere,) * 4,
        scratch_shapes=scratch,
        compiler_params=pltpu.CompilerParams(
            collective_id=0, has_side_effects=True, vmem_limit_bytes=40 * 1024 * 1024
        ),
    )(queries, key_rows, value_rows, layer_grad, w_out, block_order, doc_lengths)


def solution(mesh):
    return jax.shard_map(
        local,
        mesh=mesh,
        in_specs=(
            P("seq", "heads"),
            P("seq", None),
            P("seq", None),
            P("seq", "heads"),
            P(None, "heads"),
            P(),
            P(),
        ),
        out_specs=(P("seq", "heads"), P("seq", None), P("seq", None), P("seq", "heads")),
        check_vma=False,
    )
```

time: 596 us -> 62.5 us (0.10)
  waiting for transfers between devices: 188 us -> 0 us
  starting transfers between devices: 143 us -> 0 us
  loops' own time: 121 us -> 0 us
  other arithmetic: 57.7 us -> 0 us
  Pallas kernels: 0 us -> 52.6 us
  local copies, waits for them, and re-layouts: 39.4 us -> 9.06 us
  matrix products: 24.3 us -> 0 us
  between operations: 20.8 us -> 0.66 us
    psum x1 -> x0, waiting for transfers between devices: 176 us -> none  [local(): lax.psum(placed_keys.astype(jnp.bfloat16), 'heads').astype(jnp.float32)]
    ppermute x136 -> x0, starting transfers between devices: 143 us -> none  [shifted(): lax.ppermute(array, axis, [(i, (i + by) % size) for i in range(size)])]
    another operation x130 -> x0, loops' own time: 121 us -> none  [the longest x1 59.2 us: local(): lax.fori_loop(1, cycle_size, backward_hop, (bundle + (jnp.concatenate(que...]
    pallas_call x0 -> x1, Pallas kernels: none -> 52.6 us  [local(): pl.pallas_call(make_kernel(n_seq), out_shape=(jax.ShapeDtypeStruct(querie...]
    reduce_or x31 -> x0, other arithmetic: 26.7 us -> none  [the longest x16 13.5 us: backward_tile(): jnp.any(allowed)]
    dot_general x114 -> x0, matrix products: 24.3 us -> none  [the longest x50 11 us: contract_last(): lax.dot_general(left, right, (((1,), (1,)), ((), ())), preferred_element_...]
    dynamic_slice x31 -> x0, local copies, waits for them, and re-layouts: 19.8 us -> none  [slot_rows(): leading = lax.dynamic_slice_in_dim(block_order, slot_index, 1)[0]]
    add x81 -> x0, other arithmetic: 13.7 us -> none  [the longest x19 12.7 us: forward_update(): row_sum = row_sum * factor + jnp.sum(weights, axis=1)]
  transfers between devices with their start and end apart: 138 -> 0, of which waited for: 10 -> 0; matrix products, arithmetic and copies ran while one was open for 16% -> 0% of each run, Pallas kernels for 0% -> 0%
where the time goes in v1:
time: 62.5 us; the launch traced here: 62.3 us
  Pallas kernels  52.6 us (84%)
  local copies, waits for them, and re-layouts  9.06 us (14%)
  between operations  0.66 us (1%)
    pallas_call x1, Pallas kernels, local(): pl.pallas_call(make_kernel(n_seq), out_shape=(jax.ShapeDtypeStruct(querie...  52.6 us
    unnamed x18, local copies, waits for them, and re-layouts  9.06 us

profile of v1, /device:TPU:1, one launch (start us, length us, event | category | flops | bytes accessed | tf_op | source)
XLA Modules:
  0.0 62.3 jit_solution(4581491449247520219)
XLA Ops:
  0.6 0.0 copy-start
  0.6 1.6 %copy-done = bf16[2048,512]{1,0:T(8,128)(2,1)S(1)} copy-done((bf16[2048,512]{1,0:T(8,128)(2,1)S(1)}, bf16[2048,512]{1,0:T(8,128)(2,1)}, u32[]{:S(2)}) %copy-start) | copy-done | bytes 2097176
  2.2 0.0 copy-start.1
  2.2 0.9 %copy-done.1 = bf16[256,512]{1,0:T(8,128)(2,1)S(1)} copy-done((bf16[256,512]{1,0:T(8,128)(2,1)S(1)}, bf16[256,512]{1,0:T(8,128)(2,1)}, u32[]{:S(2)}) %copy-start.1) | copy-done | bytes 262168
  3.2 0.0 copy-start.2
  3.2 0.9 %copy-done.2 = bf16[256,256]{1,0:T(8,128)(2,1)S(1)} copy-done((bf16[256,256]{1,0:T(8,128)(2,1)S(1)}, bf16[256,256]{1,0:T(8,128)(2,1)}, u32[]{:S(2)}) %copy-start.2) | copy-done | bytes 131096
  4.1 0.0 copy-start.3
  4.1 0.9 %copy-done.3 = bf16[256,256]{1,0:T(8,128)(2,1)S(1)} copy-done((bf16[256,256]{1,0:T(8,128)(2,1)S(1)}, bf16[256,256]{1,0:T(8,128)(2,1)}, u32[]{:S(2)}) %copy-start.3) | copy-done | bytes 131096
  5.0 0.0 copy-start.4
  5.0 0.8 %copy-done.4 = bf16[256,128]{1,0:T(8,128)(2,1)S(1)} copy-done((bf16[256,128]{1,0:T(8,128)(2,1)S(1)}, bf16[256,128]{1,0:T(8,128)(2,1)}, u32[]{:S(2)}) %copy-start.4) | copy-done | bytes 65560
  5.8 0.0 copy-start.5
  5.8 0.7 %copy-done.5 = s32[32]{0:T(128)S(1)} copy-done((s32[32]{0:T(128)S(1)}, s32[32]{0:T(128)}, u32[]{:S(2)}) %copy-start.5) | copy-done | bytes 152
  6.5 0.0 copy-start.6
  6.5 0.7 %copy-done.6 = s32[4]{0:T(128)S(1)} copy-done((s32[4]{0:T(128)S(1)}, s32[4]{0:T(128)}, u32[]{:S(2)}) %copy-start.6) | copy-done | bytes 40
  7.1 52.6 %shard_map.102 = (bf16[256,128]{1,0:T(8,128)(2,1)S(1)}, bf16[256,256]{1,0:T(8,128)(2,1)S(1)}, bf16[256,256]{1,0:T(8,128)(2,1)S(1)}, bf16[256,128]{1,0:T(8,128)(2,1)S(1)}) custom-call(bf16[256,128]{1,0:T(8,128)(2,1)S(1)} %copy-done.4, bf16[256,256]{1,0:T(8,128)(2,1)S(1)} %copy-done.2, bf16[256,256]{1,0:T(8,128)(2,1)S(1)} %copy-done.3, ...), custom_call_target="tpu_custom_call" | custom-call | tf_op jit(solution)/shard_map/pallas_call | solution.py:444
  59.7 0.6 %copy.15 = bf16[256,128]{1,0:T(8,128)(2,1)} copy(bf16[256,128]{1,0:T(8,128)(2,1)S(1)} %get-tuple-element.8) | data formatting | bytes 131072
  60.3 0.7 %copy.16 = bf16[256,256]{1,0:T(8,128)(2,1)} copy(bf16[256,256]{1,0:T(8,128)(2,1)S(1)} %get-tuple-element.9) | data formatting | bytes 262144
  61.0 0.7 %copy.17 = bf16[256,256]{1,0:T(8,128)(2,1)} copy(bf16[256,256]{1,0:T(8,128)(2,1)S(1)} %get-tuple-element.10) | data formatting | bytes 262144
  61.6 0.6 %copy.18 = bf16[256,128]{1,0:T(8,128)(2,1)} copy(bf16[256,128]{1,0:T(8,128)(2,1)S(1)} %get-tuple-element.11) | data formatting | bytes 131072
Async XLA Ops:
  0.6 1.6 %copy-start = (bf16[2048,512]{1,0:T(8,128)(2,1)S(1)}, bf16[2048,512]{1,0:T(8,128)(2,1)}, u32[]{:S(2)}) copy-start(bf16[2048,512]{1,0:T(8,128)(2,1)} %w_hbm.1) | copy-start | bytes 6291460
  2.2 0.9 %copy-start.1 = (bf16[256,512]{1,0:T(8,128)(2,1)S(1)}, bf16[256,512]{1,0:T(8,128)(2,1)}, u32[]{:S(2)}) copy-start(bf16[256,512]{1,0:T(8,128)(2,1)} %lg_hbm.1) | copy-start | bytes 786436
  3.2 0.9 %copy-start.2 = (bf16[256,256]{1,0:T(8,128)(2,1)S(1)}, bf16[256,256]{1,0:T(8,128)(2,1)}, u32[]{:S(2)}) copy-start(bf16[256,256]{1,0:T(8,128)(2,1)} %k_hbm.1) | copy-start | bytes 393220
  4.1 0.9 %copy-start.3 = (bf16[256,256]{1,0:T(8,128)(2,1)S(1)}, bf16[256,256]{1,0:T(8,128)(2,1)}, u32[]{:S(2)}) copy-start(bf16[256,256]{1,0:T(8,128)(2,1)} %v_hbm.1) | copy-start | bytes 393220
  5.0 0.8 %copy-start.4 = (bf16[256,128]{1,0:T(8,128)(2,1)S(1)}, bf16[256,128]{1,0:T(8,128)(2,1)}, u32[]{:S(2)}) copy-start(bf16[256,128]{1,0:T(8,128)(2,1)} %q_hbm.1) | copy-start | bytes 196612
  5.8 0.7 %copy-start.5 = (s32[32]{0:T(128)S(1)}, s32[32]{0:T(128)}, u32[]{:S(2)}) copy-start(s32[32]{0:T(128)} %bo.1) | copy-start | bytes 388
  6.5 0.7 %copy-start.6 = (s32[4]{0:T(128)S(1)}, s32[4]{0:T(128)}, u32[]{:S(2)}) copy-start(s32[4]{0:T(128)} %dl.1) | copy-start | bytes 52

commit v2 on v1

v2 whole, which is shorter than its diff:
```python
import math

import jax
import jax.numpy as jnp
from jax import lax
from jax.experimental import pallas as pl
from jax.experimental.pallas import tpu as pltpu
from jax.sharding import PartitionSpec as P

GROUP = 8
DH = 128
ROWS = 256
MESH = pl.DeviceIdType.MESH
F32 = jnp.float32
BF16 = jnp.bfloat16
NEG = -1e30


def contract_last(left, right):
    return lax.dot_general(
        left, right, (((1,), (1,)), ((), ())), preferred_element_type=F32
    )


def matmul(left, right):
    return jnp.dot(left, right, preferred_element_type=F32)


def make_kernel(n_seq):
    part = ROWS // GROUP
    keys = n_seq * part
    n_heads = 2 * GROUP
    chips = n_heads // 2
    scale = 1.0 / math.sqrt(DH)
    scale2 = scale * math.log2(math.e)

    def kernel(
        q_hbm, k_hbm, v_hbm, lg_hbm, w_hbm, bo_hbm, dl_hbm,
        qg_out, kg_out, vg_out, hg_out,
        w_v, lg_v, q_all, do_all, k_all, v_all, kt_v, bias, bo, dl,
        mine, oth_tx, oth_rx, c1_tx, c1_rx,
        e_all, dp_all, ds_all, st_own, st_rx, d_own, d_rx, fac, dsum,
        dv_acc, dk_acc, dv_tx, dk_tx, dv_rx, dk_rx, dv_fin, dk_fin,
        dq_tx, dq_rx, qg_v,
        w_sem, ld_sem, out_sem,
        q_send, q_recv, k_send, k_recv, v_send, v_recv, oth_send, oth_recv, c1_send, c1_recv,
        do_send, do_recv, st_send, st_recv, d_send, d_recv, dq_send, dq_recv,
        dv_send, dv_recv, dk_send, dk_recv, av_send, av_recv, ak_send, ak_recv,
    ):
        h = lax.axis_index("heads")
        s = lax.axis_index("seq")
        c = h // GROUP
        j = h % GROUP
        x = j // 2
        core = h % 2
        chip = h // 2
        sib = h + 1 - 2 * core
        seq_order = sorted(range(1, n_seq), key=lambda r: abs(2 * r - n_seq))
        chip_order = (6, 2, 5, 7, 4, 1, 3, 0)
        rest = pl.ds(part, keys - part)

        def to_head(src, dst, send_sem, recv_sem, target):
            return pltpu.make_async_remote_copy(
                src_ref=src, dst_ref=dst, send_sem=send_sem, recv_sem=recv_sem,
                device_id={"heads": target}, device_id_type=MESH,
            )

        def to_seq(src, dst, send_sem, recv_sem, target):
            return pltpu.make_async_remote_copy(
                src_ref=src, dst_ref=dst, send_sem=send_sem, recv_sem=recv_sem,
                device_id={"seq": target}, device_id_type=MESH,
            )

        def await_bytes(ref, sem):
            pltpu.make_async_copy(ref, ref, sem).wait()

        row0 = pl.multiple_of(j * part, part)
        col0 = pl.multiple_of(c * DH, DH)
        own_rows = pl.ds(0, part)
        lg_load = pltpu.make_async_copy(lg_hbm, lg_v, ld_sem.at[0])
        lg_load.start()
        w_loads = []
        for step, r in enumerate(chip_order):
            target = ((chip + r) % chips) * 2
            for which, head in enumerate((target + core, target + 1 - core)):
                load = pltpu.make_async_copy(
                    w_hbm.at[pl.ds(pl.multiple_of(head * DH, DH), DH), :],
                    w_v.at[step, pl.ds(which * DH, DH), :],
                    w_sem.at[step, which],
                )
                load.start()
                w_loads.append(load)
        small_loads = [
            pltpu.make_async_copy(q_hbm, q_all.at[j], ld_sem.at[1]),
            pltpu.make_async_copy(
                k_hbm.at[pl.ds(row0, part), pl.ds(col0, DH)], k_all.at[own_rows, :], ld_sem.at[2]
            ),
            pltpu.make_async_copy(
                v_hbm.at[pl.ds(row0, part), pl.ds(col0, DH)], v_all.at[own_rows, :], ld_sem.at[3]
            ),
            pltpu.make_async_copy(bo_hbm, bo, ld_sem.at[4]),
            pltpu.make_async_copy(dl_hbm, dl, ld_sem.at[5]),
        ]
        for load in small_loads:
            load.start()

        barrier = pltpu.get_barrier_semaphore()
        for r in seq_order:
            pl.semaphore_signal(
                barrier, inc=1, device_id={"seq": (s + r) % n_seq}, device_id_type=MESH
            )
        for r in range(1, n_heads):
            pl.semaphore_signal(
                barrier, inc=1, device_id={"heads": (h + r) % n_heads}, device_id_type=MESH
            )

        lg_load.wait()
        for step in range(chips):
            w_loads[2 * step].wait()
            w_loads[2 * step + 1].wait()
            product = contract_last(lg_v[...], w_v[step])
            oth_tx[step] = product[:, DH:].astype(BF16)
            mine[step] = product[:, :DH]
        for load in small_loads:
            load.wait()
        pl.semaphore_wait(barrier, n_heads + n_seq - 2)

        oth_copies = [
            to_head(oth_tx.at[i], oth_rx.at[i], oth_send.at[i], oth_recv.at[i], sib)
            for i in range(chips)
        ]
        for copy in oth_copies:
            copy.start()

        def spread_seq(buf, send, recv):
            for r in seq_order:
                to_seq(
                    buf.at[own_rows, :], buf.at[pl.ds(r * part, part), :],
                    send, recv, (s + r) % n_seq,
                ).start()

        spread_seq(k_all, k_send, k_recv)

        c1_copies = []
        for i, r in enumerate(chip_order):
            oth_copies[i].wait_recv()
            total = mine[i] + oth_rx[i].astype(F32)
            if r == 0:
                mine[i] = total
            else:
                c1_tx[i] = total.astype(BF16)
                copy = to_head(
                    c1_tx.at[i], c1_rx.at[i], c1_send.at[i], c1_recv,
                    ((chip + r) % chips) * 2 + core,
                )
                copy.start()
                c1_copies.append(copy)

        def peer(t, q):
            return ((x - t + 4) % 4) * 2 + (core + q) % 2

        def gather_first(buf, send, recv):
            for t in (2, 1, 3):
                to_head(
                    buf.at[j], buf.at[j], send.at[2 * t], recv.at[2 * t],
                    c * GROUP + ((x + t) % 4) * 2 + core,
                ).start()
            to_head(buf.at[j], buf.at[j], send.at[1], recv.at[1], sib).start()

        def gather_wait(buf, recv, t, q):
            await_bytes(buf.at[peer(t, q)], recv.at[2 * t + q])

        def gather_pass(buf, send, recv, t):
            gather_wait(buf, recv, t, 0)
            other = peer(t, 0)
            to_head(
                buf.at[other], buf.at[other], send.at[2 * t + 1], recv.at[2 * t + 1], sib
            ).start()

        gather_first(q_all, q_send, q_recv)
        spread_seq(v_all, v_send, v_recv)

        lane = lax.broadcasted_iota(jnp.int32, (1, ROWS), 1)
        q_pos = jnp.where(
            lane < ROWS // 2,
            bo[2 * s] * (ROWS // 2) + lane,
            bo[2 * s + 1] * (ROWS // 2) + lane - ROWS // 2,
        )
        start1 = dl[0]
        start2 = start1 + dl[1]
        start3 = start2 + dl[2]
        q_begin = jnp.zeros((1, ROWS), jnp.int32)
        for begin in (start1, start2, start3):
            q_begin = jnp.maximum(q_begin, jnp.where(begin <= q_pos, begin, 0))
        for r in range(n_seq):
            slot = (s - r + n_seq) % n_seq
            base = bo[2 * slot + j // 4] * (ROWS // 2) + (j % 4) * part
            k_pos = base + lax.broadcasted_iota(jnp.int32, (part, ROWS), 0)
            allowed = (k_pos <= q_pos) & (k_pos >= q_begin)
            bias[pl.ds(r * part, part), :] = jnp.where(allowed, 0.0, NEG)

        await_bytes(k_all.at[rest, :], k_recv)
        kt_v[...] = k_all[...].astype(F32).T.astype(BF16)

        await_bytes(c1_rx, c1_recv)
        total = mine[chips - 1]
        for i in range(chips - 1):
            total = total + c1_rx[i].astype(F32)
        do_all[j] = total.astype(BF16)
        gather_first(do_all, do_send, do_recv)
        hg_copy = pltpu.make_async_copy(do_all.at[j], hg_out, out_sem.at[0])
        hg_copy.start()

        order = ((0, 0), (0, 1), (1, 0), (3, 0), (2, 0), (1, 1), (3, 1), (2, 1))

        def score_head(head):
            sc = contract_last(k_all[...], q_all[head]) * scale2 + bias[...]
            top = jnp.max(sc, axis=0, keepdims=True)
            e = jnp.exp2(sc - top)
            e_all[head] = e
            st_own[0, pl.ds(head, 1), :] = top
            st_own[1, pl.ds(head, 1), :] = jnp.sum(e, axis=0, keepdims=True)

        for t, q in order:
            if t > 0 and q == 0:
                gather_pass(q_all, q_send, q_recv, t)
            elif q == 1:
                gather_wait(q_all, q_recv, t, q)
            score_head(peer(t, q))

        def group_send(own, rx, send, recv):
            for r in (4, 3, 5, 2, 6, 1, 7):
                to_head(
                    own, rx.at[r - 1], send, recv, c * GROUP + (j + r) % GROUP
                ).start()

        group_send(st_own, st_rx, st_send, st_recv)

        await_bytes(v_all.at[rest, :], v_recv)

        def dot_head(head):
            dp = contract_last(v_all[...], do_all[head])
            dp_all[head] = dp
            d_own[pl.ds(head, 1), :] = jnp.sum(e_all[head] * dp, axis=0, keepdims=True)

        for t, q in order:
            if t > 0 and q == 0:
                gather_pass(do_all, do_send, do_recv, t)
            elif q == 1:
                gather_wait(do_all, do_recv, t, q)
            dot_head(peer(t, q))

        group_send(d_own, d_rx, d_send, d_recv)

        await_bytes(st_rx, st_recv)
        top = st_own[0]
        for r in range(GROUP - 1):
            top = jnp.maximum(top, st_rx[r, 0])
        own_fac = jnp.exp2(st_own[0] - top)
        norm = st_own[1] * own_fac
        for r in range(GROUP - 1):
            norm = norm + st_rx[r, 1] * jnp.exp2(st_rx[r, 0] - top)
        inverse = 1.0 / norm
        own_fac = own_fac * inverse
        fac[...] = own_fac

        dv_acc[...] = jnp.zeros_like(dv_acc)
        for head in range(GROUP):
            p = (e_all[head] * fac[pl.ds(head, 1), :]).astype(BF16)
            dv_acc[...] += matmul(p, do_all[head])
        dv_tx[...] = dv_acc[...].astype(BF16)

        def scatter(tx, rx, send, recv):
            for r in seq_order:
                rows = pl.ds(r * part, part)
                to_seq(
                    tx.at[rows, :], rx.at[rows, :], send, recv, (s - r + n_seq) % n_seq
                ).start()

        scatter(dv_tx, dv_rx, dv_send, dv_recv)

        await_bytes(d_rx, d_recv)
        row_dots = d_own[...] * own_fac
        for r in range(GROUP - 1):
            row_dots = row_dots + d_rx[r] * (jnp.exp2(st_rx[r, 0] - top) * inverse)
        dsum[...] = row_dots

        dk_acc[...] = jnp.zeros_like(dk_acc)
        for head in range(GROUP):
            p = e_all[head] * fac[pl.ds(head, 1), :]
            ds = (p * (dp_all[head] - dsum[pl.ds(head, 1), :])).astype(BF16)
            ds_all[head] = ds
            dk_acc[...] += matmul(ds, q_all[head])
        dk_tx[...] = (dk_acc[...] * scale).astype(BF16)
        scatter(dk_tx, dk_rx, dk_send, dk_recv)

        for t, q in ((2, 0), (2, 1), (1, 0), (1, 1), (3, 0), (3, 1), (0, 1), (0, 0)):
            head = peer(t, q)
            dq_tx[head] = (matmul(kt_v[...], ds_all[head]) * scale).astype(BF16)
            slot = 2 * t + q - 1
            if slot >= 0:
                to_head(
                    dq_tx.at[head], dq_rx.at[slot], dq_send.at[slot], dq_recv, c * GROUP + head
                ).start()

        head_order = (12, 13, 11, 4, 5, 3, 10, 14, 6, 2, 9, 8, 7, 15, 1)

        def finish(tx, rx, fin, out, recv, all_send, all_recv, own_sem):
            await_bytes(rx.at[rest, :], recv)
            summed = tx[own_rows, :].astype(F32)
            for r in range(1, n_seq):
                summed = summed + rx[pl.ds(r * part, part), :].astype(F32)
            fin[...] = summed.astype(BF16)
            place = out.at[pl.ds(row0, part), pl.ds(col0, DH)]
            for r in head_order:
                to_head(fin, place, all_send, all_recv, (h + r) % n_heads).start()
            copy = pltpu.make_async_copy(fin, place, own_sem)
            copy.start()
            return copy

        vg_copy = finish(dv_tx, dv_rx, dv_fin, vg_out, dv_recv, av_send, av_recv, out_sem.at[1])
        kg_copy = finish(dk_tx, dk_rx, dk_fin, kg_out, dk_recv, ak_send, ak_recv, out_sem.at[2])

        await_bytes(dq_rx, dq_recv)
        query_sum = dq_tx[j].astype(F32)
        for r in range(GROUP - 1):
            query_sum = query_sum + dq_rx[r].astype(F32)
        qg_v[...] = query_sum.T.astype(BF16)
        qg_copy = pltpu.make_async_copy(qg_v, qg_out, out_sem.at[3])
        qg_copy.start()

        for slot in range(1, 2 * 4):
            await_bytes(q_all.at[0], q_send.at[slot])
            await_bytes(do_all.at[0], do_send.at[slot])
        for buf, send in ((k_all, k_send), (v_all, v_send), (dv_tx, dv_send), (dk_tx, dk_send)):
            await_bytes(buf.at[rest, :], send)
        for copy in oth_copies:
            copy.wait_send()
        for copy in c1_copies:
            copy.wait_send()
        await_bytes(st_rx, st_send)
        await_bytes(d_rx, d_send)
        for slot in range(GROUP - 1):
            await_bytes(dq_tx.at[0], dq_send.at[slot])
        spread = (n_heads - 1) * part
        for sem in (av_send, ak_send, av_recv, ak_recv):
            await_bytes(q_all.at[pl.ds(0, 5), pl.ds(0, spread // 5), :], sem)
        for copy in (hg_copy, qg_copy, vg_copy, kg_copy):
            copy.wait()

    return kernel


def local(queries, key_rows, value_rows, layer_grad, w_out, block_order, doc_lengths):
    n_seq = lax.axis_size("seq")
    part = ROWS // GROUP
    keys = n_seq * part
    depth = layer_grad.shape[1]
    chips = GROUP
    vmem = pltpu.VMEM
    dma = pltpu.SemaphoreType.DMA
    scratch = [
        vmem((chips, 2 * DH, depth), BF16),
        vmem((ROWS, depth), BF16),
        vmem((GROUP, ROWS, DH), BF16),
        vmem((GROUP, ROWS, DH), BF16),
        vmem((keys, DH), BF16),
        vmem((keys, DH), BF16),
        vmem((DH, keys), BF16),
        vmem((keys, ROWS), F32),
        pltpu.SMEM(block_order.shape, jnp.int32),
        pltpu.SMEM(doc_lengths.shape, jnp.int32),
        vmem((chips, ROWS, DH), F32),
        vmem((chips, ROWS, DH), BF16),
        vmem((chips, ROWS, DH), BF16),
        vmem((chips - 1, ROWS, DH), BF16),
        vmem((chips - 1, ROWS, DH), BF16),
        vmem((GROUP, keys, ROWS), F32),
        vmem((GROUP, keys, ROWS), F32),
        vmem((GROUP, keys, ROWS), BF16),
        vmem((2, GROUP, ROWS), F32),
        vmem((GROUP - 1, 2, GROUP, ROWS), F32),
        vmem((GROUP, ROWS), F32),
        vmem((GROUP - 1, GROUP, ROWS), F32),
        vmem((GROUP, ROWS), F32),
        vmem((GROUP, ROWS), F32),
        vmem((keys, DH), F32),
        vmem((keys, DH), F32),
        vmem((keys, DH), BF16),
        vmem((keys, DH), BF16),
        vmem((keys, DH), BF16),
        vmem((keys, DH), BF16),
        vmem((part, DH), BF16),
        vmem((part, DH), BF16),
        vmem((GROUP, DH, ROWS), BF16),
        vmem((GROUP - 1, DH, ROWS), BF16),
        vmem((ROWS, DH), BF16),
        dma((chips, 2)),
        dma((6,)),
        dma((4,)),
        dma((8,)),
        dma((8,)),
        dma,
        dma,
        dma,
        dma,
        dma((chips,)),
        dma((chips,)),
        dma((chips - 1,)),
        dma,
        dma((8,)),
        dma((8,)),
        dma,
        dma,
        dma,
        dma,
        dma((GROUP - 1,)),
        dma,
        dma,
        dma,
        dma,
        dma,
        dma,
        dma,
        dma,
        dma,
    ]
    anywhere = pl.BlockSpec(memory_space=pl.ANY)
    return pl.pallas_call(
        make_kernel(n_seq),
        out_shape=(
            jax.ShapeDtypeStruct(queries.shape, BF16),
            jax.ShapeDtypeStruct(key_rows.shape, BF16),
            jax.ShapeDtypeStruct(value_rows.shape, BF16),
            jax.ShapeDtypeStruct(queries.shape, BF16),
        ),
        in_specs=[anywhere] * 7,
        out_specs=(anywhere,) * 4,
        scratch_shapes=scratch,
        compiler_params=pltpu.CompilerParams(
            collective_id=0, has_side_effects=True, vmem_limit_bytes=58 * 1024 * 1024
        ),
    )(queries, key_rows, value_rows, layer_grad, w_out, block_order, doc_lengths)


def solution(mesh):
    return jax.shard_map(
        local,
        mesh=mesh,
        in_specs=(
            P("seq", "heads"),
            P("seq", None),
            P("seq", None),
            P("seq", "heads"),
            P(None, "heads"),
            P(),
            P(),
        ),
        out_specs=(P("seq", "heads"), P("seq", None), P("seq", None), P("seq", "heads")),
        check_vma=False,
    )
```

time: 62.5 us -> 54.8 us (0.88)
  Pallas kernels: 52.6 us -> 47.9 us
  local copies, waits for them, and re-layouts: 9.06 us -> 6.08 us
    pallas_call x1, Pallas kernels: 52.6 us -> 47.9 us  [local(): pl.pallas_call(make_kernel(n_seq), out_shape=(jax.ShapeDtypeStruct(querie...]
    unnamed x18 -> x4, local copies, waits for them, and re-layouts: 9.06 us -> 6.08 us
where the time goes in v2:
time: 54.8 us; the launch traced here: 54.6 us
  Pallas kernels  47.9 us (87%)
  local copies, waits for them, and re-layouts  6.08 us (11%)
  between operations  0.64 us (1%)
    pallas_call x1, Pallas kernels, local(): pl.pallas_call(make_kernel(n_seq), out_shape=(jax.ShapeDtypeStruct(querie...  47.9 us
    unnamed x4, local copies, waits for them, and re-layouts  6.08 us

profile of v2, /device:TPU:1, one launch (start us, length us, event | category | flops | bytes accessed | tf_op | source)
XLA Modules:
  0.0 54.6 jit_solution(5378536126773221664)
XLA Ops:
  0.6 47.9 %shard_map.102 = (bf16[256,128]{1,0:T(8,128)(2,1)}, bf16[256,256]{1,0:T(8,128)(2,1)}, bf16[256,256]{1,0:T(8,128)(2,1)}, bf16[256,128]{1,0:T(8,128)(2,1)}) custom-call(bf16[256,128]{1,0:T(8,128)(2,1)} %q_hbm.1, bf16[256,256]{1,0:T(8,128)(2,1)} %k_hbm.1, bf16[256,256]{1,0:T(8,128)(2,1)} %v_hbm.1, bf16[256,512]{1,0:T(8,128)(2,1)} %lg_hbm.1, ...), custom_call_target="tpu_custom_call" | custom-call | tf_op jit(solution)/shard_map/pallas_call | solution.py:429
  48.5 1.5 %copy.15 = bf16[256,128]{1,0:T(8,128)(2,1)} copy(bf16[256,128]{1,0:T(8,128)(2,1)} %get-tuple-element.8) | data formatting | bytes 131072
  50.0 1.6 %copy.16 = bf16[256,256]{1,0:T(8,128)(2,1)} copy(bf16[256,256]{1,0:T(8,128)(2,1)} %get-tuple-element.9) | data formatting | bytes 262144
  51.5 1.6 %copy.17 = bf16[256,256]{1,0:T(8,128)(2,1)} copy(bf16[256,256]{1,0:T(8,128)(2,1)} %get-tuple-element.10) | data formatting | bytes 262144
  53.1 1.5 %copy.18 = bf16[256,128]{1,0:T(8,128)(2,1)} copy(bf16[256,128]{1,0:T(8,128)(2,1)} %get-tuple-element.11) | data formatting | bytes 131072

commit v3 on v2

--- a/solution.py
+++ b/solution.py
@@ -8,6 +8,7 @@
 from jax.sharding import PartitionSpec as P
 
 GROUP = 8
+EARLY = 3
 DH = 128
 ROWS = 256
 MESH = pl.DeviceIdType.MESH
@@ -41,10 +42,10 @@
         mine, oth_tx, oth_rx, c1_tx, c1_rx,
         e_all, dp_all, ds_all, st_own, st_rx, d_own, d_rx, fac, dsum,
         dv_acc, dk_acc, dv_tx, dk_tx, dv_rx, dk_rx, dv_fin, dk_fin,
-        dq_tx, dq_rx, qg_v,
+        pair_tx, pair_rx, dq_own, dq_tx, dq_rx, qg_v,
         w_sem, ld_sem, out_sem,
         q_send, q_recv, k_send, k_recv, v_send, v_recv, oth_send, oth_recv, c1_send, c1_recv,
-        do_send, do_recv, st_send, st_recv, d_send, d_recv, dq_send, dq_recv,
+        do_send, do_recv, st_send, st_recv, d_send, d_recv, pair_send, pair_recv, dq_send, dq_recv,
         dv_send, dv_recv, dk_send, dk_recv, av_send, av_recv, ak_send, ak_recv,
     ):
         h = lax.axis_index("heads")
@@ -81,15 +82,22 @@
         lg_load.start()
         w_loads = []
         for step, r in enumerate(chip_order):
-            target = ((chip + r) % chips) * 2
-            for which, head in enumerate((target + core, target + 1 - core)):
-                load = pltpu.make_async_copy(
-                    w_hbm.at[pl.ds(pl.multiple_of(head * DH, DH), DH), :],
-                    w_v.at[step, pl.ds(which * DH, DH), :],
-                    w_sem.at[step, which],
-                )
-                load.start()
-                w_loads.append(load)
+            first = pl.multiple_of(((chip + r) % chips) * 2 * DH, 2 * DH)
+            load = pltpu.make_async_copy(
+                w_hbm.at[pl.ds(first, 2 * DH), :], w_v.at[step], w_sem.at[step]
+            )
+            load.start()
+            w_loads.append(load)
+        barrier = pltpu.get_barrier_semaphore()
+        for r in seq_order:
+            pl.semaphore_signal(
+                barrier, inc=1, device_id={"seq": (s + r) % n_seq}, device_id_type=MESH
+            )
+        for r in range(1, n_heads):
+            pl.semaphore_signal(
+                barrier, inc=1, device_id={"heads": (h + r) % n_heads}, device_id_type=MESH
+            )
+
         small_loads = [
             pltpu.make_async_copy(q_hbm, q_all.at[j], ld_sem.at[1]),
             pltpu.make_async_copy(
@@ -104,47 +112,23 @@
         for load in small_loads:
             load.start()
 
-        barrier = pltpu.get_barrier_semaphore()
-        for r in seq_order:
-            pl.semaphore_signal(
-                barrier, inc=1, device_id={"seq": (s + r) % n_seq}, device_id_type=MESH
-            )
-        for r in range(1, n_heads):
-            pl.semaphore_signal(
-                barrier, inc=1, device_id={"heads": (h + r) % n_heads}, device_id_type=MESH
-            )
-
-        lg_load.wait()
-        for step in range(chips):
-            w_loads[2 * step].wait()
-            w_loads[2 * step + 1].wait()
-            product = contract_last(lg_v[...], w_v[step])
-            oth_tx[step] = product[:, DH:].astype(BF16)
-            mine[step] = product[:, :DH]
-        for load in small_loads:
-            load.wait()
-        pl.semaphore_wait(barrier, n_heads + n_seq - 2)
-
         oth_copies = [
             to_head(oth_tx.at[i], oth_rx.at[i], oth_send.at[i], oth_recv.at[i], sib)
             for i in range(chips)
         ]
-        for copy in oth_copies:
-            copy.start()
-
-        def spread_seq(buf, send, recv):
-            for r in seq_order:
-                to_seq(
-                    buf.at[own_rows, :], buf.at[pl.ds(r * part, part), :],
-                    send, recv, (s + r) % n_seq,
-                ).start()
-
-        spread_seq(k_all, k_send, k_recv)
-
         c1_copies = []
-        for i, r in enumerate(chip_order):
+
+        def product_step(step):
+            w_loads[step].wait()
+            product = contract_last(lg_v[...], w_v[step])
+            even, odd = product[:, :DH], product[:, DH:]
+            oth_tx[step] = jnp.where(core == 0, odd, even).astype(BF16)
+            mine[step] = jnp.where(core == 0, even, odd)
+
+        def pair_step(i):
             oth_copies[i].wait_recv()
             total = mine[i] + oth_rx[i].astype(F32)
+            r = chip_order[i]
             if r == 0:
                 mine[i] = total
             else:
@@ -156,15 +140,32 @@
                 copy.start()
                 c1_copies.append(copy)
 
+        lg_load.wait()
+        for step in range(EARLY):
+            product_step(step)
+        for load in small_loads:
+            load.wait()
+        pl.semaphore_wait(barrier, n_heads + n_seq - 2)
+        for i in range(EARLY):
+            oth_copies[i].start()
+
         def peer(t, q):
             return ((x - t + 4) % 4) * 2 + (core + q) % 2
 
-        def gather_first(buf, send, recv):
-            for t in (2, 1, 3):
-                to_head(
-                    buf.at[j], buf.at[j], send.at[2 * t], recv.at[2 * t],
-                    c * GROUP + ((x + t) % 4) * 2 + core,
-                ).start()
+        def gather_step(buf, send, recv, t):
+            to_head(
+                buf.at[j], buf.at[j], send.at[2 * t], recv.at[2 * t],
+                c * GROUP + ((x + t) % 4) * 2 + core,
+            ).start()
+
+        def gather_far(buf, send, recv):
+            gather_step(buf, send, recv, 2)
+
+        def gather_near(buf, send, recv):
+            gather_step(buf, send, recv, 1)
+            gather_step(buf, send, recv, 3)
+
+        def gather_sibling(buf, send, recv):
             to_head(buf.at[j], buf.at[j], send.at[1], recv.at[1], sib).start()
 
         def gather_wait(buf, recv, t, q):
@@ -177,7 +178,25 @@
                 buf.at[other], buf.at[other], send.at[2 * t + 1], recv.at[2 * t + 1], sib
             ).start()
 
-        gather_first(q_all, q_send, q_recv)
+        def spread_seq(buf, send, recv):
+            for r in seq_order:
+                to_seq(
+                    buf.at[own_rows, :], buf.at[pl.ds(r * part, part), :],
+                    send, recv, (s + r) % n_seq,
+                ).start()
+
+        gather_near(q_all, q_send, q_recv)
+        spread_seq(k_all, k_send, k_recv)
+
+        for i in range(EARLY, chips):
+            product_step(i)
+            oth_copies[i].start()
+            pair_step(i - EARLY)
+        for i in range(chips - EARLY, chips):
+            pair_step(i)
+
+        gather_far(q_all, q_send, q_recv)
+        gather_sibling(q_all, q_send, q_recv)
         spread_seq(v_all, v_send, v_recv)
 
         lane = lax.broadcasted_iota(jnp.int32, (1, ROWS), 1)
@@ -202,14 +221,11 @@
         await_bytes(k_all.at[rest, :], k_recv)
         kt_v[...] = k_all[...].astype(F32).T.astype(BF16)
 
-        await_bytes(c1_rx, c1_recv)
-        total = mine[chips - 1]
-        for i in range(chips - 1):
-            total = total + c1_rx[i].astype(F32)
-        do_all[j] = total.astype(BF16)
-        gather_first(do_all, do_send, do_recv)
-        hg_copy = pltpu.make_async_copy(do_all.at[j], hg_out, out_sem.at[0])
-        hg_copy.start()
+        def group_send(own, rx, send, recv):
+            for r in (4, 3, 5, 2, 6, 1, 7):
+                to_head(
+                    own, rx.at[r - 1], send, recv, c * GROUP + (j + r) % GROUP
+                ).start()
 
         order = ((0, 0), (0, 1), (1, 0), (3, 0), (2, 0), (1, 1), (3, 1), (2, 1))
 
@@ -221,18 +237,26 @@
             st_own[0, pl.ds(head, 1), :] = top
             st_own[1, pl.ds(head, 1), :] = jnp.sum(e, axis=0, keepdims=True)
 
-        for t, q in order:
-            if t > 0 and q == 0:
-                gather_pass(q_all, q_send, q_recv, t)
-            elif q == 1:
-                gather_wait(q_all, q_recv, t, q)
-            score_head(peer(t, q))
-
-        def group_send(own, rx, send, recv):
-            for r in (4, 3, 5, 2, 6, 1, 7):
-                to_head(
-                    own, rx.at[r - 1], send, recv, c * GROUP + (j + r) % GROUP
-                ).start()
+        def score_steps(steps):
+            for t, q in steps:
+                if t > 0 and q == 0:
+                    gather_pass(q_all, q_send, q_recv, t)
+                elif q == 1:
+                    gather_wait(q_all, q_recv, t, q)
+                score_head(peer(t, q))
+
+        await_bytes(c1_rx, c1_recv)
+        total = mine[chips - 1]
+        for i in range(chips - 1):
+            total = total + c1_rx[i].astype(F32)
+        do_all[j] = total.astype(BF16)
+        gather_far(do_all, do_send, do_recv)
+        gather_near(do_all, do_send, do_recv)
+        gather_sibling(do_all, do_send, do_recv)
+        hg_copy = pltpu.make_async_copy(do_all.at[j], hg_out, out_sem.at[0])
+        hg_copy.start()
+
+        score_steps(order)
 
         group_send(st_own, st_rx, st_send, st_recv)
 
@@ -294,14 +318,33 @@
         dk_tx[...] = (dk_acc[...] * scale).astype(BF16)
         scatter(dk_tx, dk_rx, dk_send, dk_recv)
 
-        for t, q in ((2, 0), (2, 1), (1, 0), (1, 1), (3, 0), (3, 1), (0, 1), (0, 0)):
+        def query_part(t, q):
             head = peer(t, q)
-            dq_tx[head] = (matmul(kt_v[...], ds_all[head]) * scale).astype(BF16)
-            slot = 2 * t + q - 1
-            if slot >= 0:
-                to_head(
-                    dq_tx.at[head], dq_rx.at[slot], dq_send.at[slot], dq_recv, c * GROUP + head
-                ).start()
+            return matmul(kt_v[...], ds_all[head]) * scale
+
+        pair_copies = []
+        for t in (2, 1, 3, 0):
+            pair_tx[t] = query_part(t, 1).astype(BF16)
+            copy = to_head(
+                pair_tx.at[t], pair_rx.at[t], pair_send.at[t], pair_recv.at[t], sib
+            )
+            copy.start()
+            pair_copies.append(copy)
+        dq_copies = []
+        for t, copy in zip((2, 1, 3, 0), pair_copies):
+            part_sum = query_part(t, 0)
+            copy.wait_recv()
+            part_sum = part_sum + pair_rx[t].astype(F32)
+            if t == 0:
+                dq_own[...] = part_sum
+            else:
+                dq_tx[t - 1] = part_sum.astype(BF16)
+                copy = to_head(
+                    dq_tx.at[t - 1], dq_rx.at[t - 1], dq_send.at[t - 1], dq_recv,
+                    c * GROUP + peer(t, 0),
+                )
+                copy.start()
+                dq_copies.append(copy)
 
         head_order = (12, 13, 11, 4, 5, 3, 10, 14, 6, 2, 9, 8, 7, 15, 1)
 
@@ -322,8 +365,8 @@
         kg_copy = finish(dk_tx, dk_rx, dk_fin, kg_out, dk_recv, ak_send, ak_recv, out_sem.at[2])
 
         await_bytes(dq_rx, dq_recv)
-        query_sum = dq_tx[j].astype(F32)
-        for r in range(GROUP - 1):
+        query_sum = dq_own[...]
+        for r in range(3):
             query_sum = query_sum + dq_rx[r].astype(F32)
         qg_v[...] = query_sum.T.astype(BF16)
         qg_copy = pltpu.make_async_copy(qg_v, qg_out, out_sem.at[3])
@@ -332,23 +375,36 @@
         for slot in range(1, 2 * 4):
             await_bytes(q_all.at[0], q_send.at[slot])
             await_bytes(do_all.at[0], do_send.at[slot])
-        for buf, send in ((k_all, k_send), (v_all, v_send), (dv_tx, dv_send), (dk_tx, dk_send)):
+        for buf, send in ((k_all, k_send), (v_all, v_send)):
             await_bytes(buf.at[rest, :], send)
-        for copy in oth_copies:
-            copy.wait_send()
-        for copy in c1_copies:
+        for copy in oth_copies + c1_copies + pair_copies:
             copy.wait_send()
         await_bytes(st_rx, st_send)
         await_bytes(d_rx, d_send)
-        for slot in range(GROUP - 1):
-            await_bytes(dq_tx.at[0], dq_send.at[slot])
+        hg_copy.wait()
+
+        for buf, send in ((dv_tx, dv_send), (dk_tx, dk_send)):
+            await_bytes(buf.at[rest, :], send)
+        for copy in dq_copies:
+            copy.wait_send()
         spread = (n_heads - 1) * part
         for sem in (av_send, ak_send, av_recv, ak_recv):
             await_bytes(q_all.at[pl.ds(0, 5), pl.ds(0, spread // 5), :], sem)
-        for copy in (hg_copy, qg_copy, vg_copy, kg_copy):
+        for copy in (qg_copy, vg_copy, kg_copy):
             copy.wait()
 
     return kernel
+
+
+def place_results(*refs):
+    sems = refs[-1]
+    copies = [
+        pltpu.make_async_copy(refs[i], refs[4 + i], sems.at[i]) for i in range(4)
+    ]
+    for copy in copies:
+        copy.start()
+    for copy in copies:
+        copy.wait()
 
 
 def local(queries, key_rows, value_rows, layer_grad, w_out, block_order, doc_lengths):
@@ -392,10 +448,13 @@
         vmem((keys, DH), BF16),
         vmem((part, DH), BF16),
         vmem((part, DH), BF16),
-        vmem((GROUP, DH, ROWS), BF16),
-        vmem((GROUP - 1, DH, ROWS), BF16),
+        vmem((4, DH, ROWS), BF16),
+        vmem((4, DH, ROWS), BF16),
+        vmem((DH, ROWS), F32),
+        vmem((3, DH, ROWS), BF16),
+        vmem((3, DH, ROWS), BF16),
         vmem((ROWS, DH), BF16),
-        dma((chips, 2)),
+        dma((chips,)),
         dma((6,)),
         dma((4,)),
         dma((8,)),
@@ -414,7 +473,9 @@
         dma,
         dma,
         dma,
-        dma((GROUP - 1,)),
+        dma((4,)),
+        dma((4,)),
+        dma((3,)),
         dma,
         dma,
         dma,
@@ -426,14 +487,15 @@
         dma,
     ]
     anywhere = pl.BlockSpec(memory_space=pl.ANY)
-    return pl.pallas_call(
+    shapes = (
+        jax.ShapeDtypeStruct(queries.shape, BF16),
+        jax.ShapeDtypeStruct(key_rows.shape, BF16),
+        jax.ShapeDtypeStruct(value_rows.shape, BF16),
+        jax.ShapeDtypeStruct(queries.shape, BF16),
+    )
+    results = pl.pallas_call(
         make_kernel(n_seq),
-        out_shape=(
-            jax.ShapeDtypeStruct(queries.shape, BF16),
-            jax.ShapeDtypeStruct(key_rows.shape, BF16),
-            jax.ShapeDtypeStruct(value_rows.shape, BF16),
-            jax.ShapeDtypeStruct(queries.shape, BF16),
-        ),
+        out_shape=tuple(pltpu.VMEM(shape.shape, BF16) for shape in shapes),
         in_specs=[anywhere] * 7,
         out_specs=(anywhere,) * 4,
         scratch_shapes=scratch,
@@ -441,6 +503,14 @@
             collective_id=0, has_side_effects=True, vmem_limit_bytes=58 * 1024 * 1024
         ),
     )(queries, key_rows, value_rows, layer_grad, w_out, block_order, doc_lengths)
+    return pl.pallas_call(
+        place_results,
+        out_shape=shapes,
+        in_specs=[anywhere] * 4,
+        out_specs=(anywhere,) * 4,
+        scratch_shapes=[dma((4,))],
+        compiler_params=pltpu.CompilerParams(vmem_limit_bytes=58 * 1024 * 1024),
+    )(*[pltpu.with_memory_space_constraint(part_out, pltpu.VMEM) for part_out in results])
 
 
 def solution(mesh):

time: 54.8 us -> 48.9 us (0.89)
  local copies, waits for them, and re-layouts: 6.08 us -> 0 us
    unnamed x4 -> x0, local copies, waits for them, and re-layouts: 6.08 us -> none
    pallas_call x1 -> x2, Pallas kernels: 47.9 us -> 48.2 us  [the longest x1 47.4 us: local(): pl.pallas_call(make_kernel(n_seq), out_shape=tuple((pltpu.VMEM(shape.shap...]
where the time goes in v3:
time: 48.9 us; the launch traced here: 48.8 us
  Pallas kernels  48.2 us (99%)
  between operations  0.64 us (1%)
    pallas_call x1, Pallas kernels, local(): pl.pallas_call(make_kernel(n_seq), out_shape=tuple((pltpu.VMEM(shape.shap...  47.4 us

profile of v3, /device:TPU:1, one launch (start us, length us, event | category | flops | bytes accessed | tf_op | source)
XLA Modules:
  0.0 48.8 jit_solution(14257602824057206286)
XLA Ops:
  0.6 47.4 %shard_map.102 = (bf16[256,128]{1,0:T(8,128)(2,1)S(1)}, bf16[256,256]{1,0:T(8,128)(2,1)S(1)}, bf16[256,256]{1,0:T(8,128)(2,1)S(1)}, bf16[256,128]{1,0:T(8,128)(2,1)S(1)}) custom-call(bf16[256,128]{1,0:T(8,128)(2,1)} %q_hbm.1, bf16[256,256]{1,0:T(8,128)(2,1)} %k_hbm.1, bf16[256,256]{1,0:T(8,128)(2,1)} %v_hbm.1, bf16[256,512]{1,0:T(8,128)(2,1)} %lg_hbm.1, ...), custom_call_target="tpu_custom_call" | custom-call | tf_op jit(solution)/shard_map/pallas_call | solution.py:496
  48.0 0.8 %shard_map.103 = (bf16[256,128]{1,0:T(8,128)(2,1)}, bf16[256,256]{1,0:T(8,128)(2,1)}, bf16[256,256]{1,0:T(8,128)(2,1)}, bf16[256,128]{1,0:T(8,128)(2,1)}) custom-call(bf16[256,128]{1,0:T(8,128)(2,1)S(1)} %get-tuple-element.8.refs_0_, bf16[256,256]{1,0:T(8,128)(2,1)S(1)} %get-tuple-element.9.refs_1_, bf16[256,256]{1,0:T(8,128)(2,1)S(1)} %get-tuple-element.10.refs_2_, ...), custom_call_target="tpu_custom_call" | custom-call | tf_op jit(solution)/shard_map/pallas_call | solution.py:506

commit v4 on v3

v4 whole, which is shorter than its diff:
```python
import math

import jax
import jax.numpy as jnp
from jax import lax
from jax.experimental import pallas as pl
from jax.experimental.pallas import tpu as pltpu
from jax.sharding import PartitionSpec as P

GROUP = 8
EARLY = 3
DH = 128
ROWS = 256
MESH = pl.DeviceIdType.MESH
F32 = jnp.float32
BF16 = jnp.bfloat16
NEG = -1e30


def contract_last(left, right):
    return lax.dot_general(
        left, right, (((1,), (1,)), ((), ())), preferred_element_type=F32
    )


def matmul(left, right):
    return jnp.dot(left, right, preferred_element_type=F32)


def make_kernel(n_seq):
    part = ROWS // GROUP
    keys = n_seq * part
    both = 2 * keys
    n_heads = 2 * GROUP
    chips = n_heads // 2
    scale = 1.0 / math.sqrt(DH)
    scale2 = scale * math.log2(math.e)

    def kernel(
        q_hbm, k_hbm, v_hbm, lg_hbm, w_hbm, bo_hbm, dl_hbm,
        qg_out, kg_out, vg_out, hg_out,
        w_v, lg_v, q_all, do_all, k_all, v_all, kt_v, bias, bo, dl,
        mine, oth_tx, oth_rx, c1_tx, c1_rx,
        e_all, dp_all, ds_all, st_own, st_rx, d_own, d_rx, fac, dsum,
        acc, half_tx, half_rx, dv_tx, dk_tx, dv_rx, dk_rx, dv_fin, dk_fin,
        dq_own, dq_tx, dq_rx, qg_v,
        w_sem, ld_sem, out_sem,
        q_send, q_recv, pair_kv_send, pair_kv_recv, sib_send, sib_recv, k_send, k_recv, v_send, v_recv, oth_send, oth_recv, c1_send, c1_recv,
        do_send, do_recv, st_send, st_recv, d_send, d_recv, half_send, half_recv, dq_send, dq_recv,
        dv_send, dv_recv, dk_send, dk_recv, av_send, av_recv, ak_send, ak_recv,
    ):
        h = lax.axis_index("heads")
        s = lax.axis_index("seq")
        c = h // GROUP
        j = h % GROUP
        x = j // 2
        core = h % 2

        def device(dy, dx, dc):
            return (((c + dy) % 2) * 4 + (x + dx) % 4) * 2 + (core + dc) % 2

        sib = h + 1 - 2 * core
        seq_order = sorted(range(1, n_seq), key=lambda r: abs(2 * r - n_seq))
        across = (2, 1, 3, 0)
        chip_order = [(dy, dx) for dy in (1, 0) for dx in across]
        head_order = [(dy, dx, dc) for dy, dx in chip_order for dc in (1, 0)][:-1]
        rest = pl.ds(part, keys - part)
        spread_rows = pl.ds(0, keys - 2 * part)

        def to_head(src, dst, send_sem, recv_sem, target):
            return pltpu.make_async_remote_copy(
                src_ref=src, dst_ref=dst, send_sem=send_sem, recv_sem=recv_sem,
                device_id={"heads": target}, device_id_type=MESH,
            )

        def to_seq(src, dst, send_sem, recv_sem, target):
            return pltpu.make_async_remote_copy(
                src_ref=src, dst_ref=dst, send_sem=send_sem, recv_sem=recv_sem,
                device_id={"seq": target}, device_id_type=MESH,
            )

        def await_bytes(ref, sem):
            pltpu.make_async_copy(ref, ref, sem).wait()

        row0 = pl.multiple_of(j * part, part)
        col0 = pl.multiple_of(c * DH, DH)
        own_rows = pl.ds(0, part)
        lg_load = pltpu.make_async_copy(lg_hbm, lg_v, ld_sem.at[0])
        lg_load.start()
        w_loads = []
        for step, (dy, dx) in enumerate(chip_order):
            first = pl.multiple_of((device(dy, dx, 0) // 2) * 2 * DH, 2 * DH)
            load = pltpu.make_async_copy(
                w_hbm.at[pl.ds(first, 2 * DH), :], w_v.at[step], w_sem.at[step]
            )
            load.start()
            w_loads.append(load)
        barrier = pltpu.get_barrier_semaphore()
        for r in seq_order:
            pl.semaphore_signal(
                barrier, inc=1, device_id={"seq": (s + r) % n_seq}, device_id_type=MESH
            )
        for r in range(1, n_heads):
            pl.semaphore_signal(
                barrier, inc=1, device_id={"heads": (h + r) % n_heads}, device_id_type=MESH
            )

        small_loads = [
            pltpu.make_async_copy(q_hbm, q_all.at[x], ld_sem.at[1]),
            pltpu.make_async_copy(
                k_hbm.at[pl.ds(row0, part), pl.ds(col0, DH)], k_all.at[own_rows, :], ld_sem.at[2]
            ),
            pltpu.make_async_copy(
                v_hbm.at[pl.ds(row0, part), pl.ds(col0, DH)], v_all.at[own_rows, :], ld_sem.at[3]
            ),
            pltpu.make_async_copy(bo_hbm, bo, ld_sem.at[4]),
            pltpu.make_async_copy(dl_hbm, dl, ld_sem.at[5]),
        ]
        for load in small_loads:
            load.start()

        oth_copies = [
            to_head(oth_tx.at[i], oth_rx.at[i], oth_send.at[i], oth_recv.at[i], sib)
            for i in range(chips)
        ]
        c1_copies = []

        def product_step(step):
            w_loads[step].wait()
            product = contract_last(lg_v[...], w_v[step])
            even, odd = product[:, :DH], product[:, DH:]
            oth_tx[step] = jnp.where(core == 0, odd, even).astype(BF16)
            mine[step] = jnp.where(core == 0, even, odd)

        def pair_step(i):
            oth_copies[i].wait_recv()
            total = mine[i] + oth_rx[i].astype(F32)
            if i == chips - 1:
                mine[i] = total
            else:
                c1_tx[i] = total.astype(BF16)
                copy = to_head(
                    c1_tx.at[i], c1_rx.at[i], c1_send.at[i], c1_recv,
                    device(*chip_order[i], 0),
                )
                copy.start()
                c1_copies.append(copy)

        lg_load.wait()
        for step in range(EARLY):
            product_step(step)
        for load in small_loads:
            load.wait()
        pl.semaphore_wait(barrier, n_heads + n_seq - 2)
        for i in range(EARLY):
            oth_copies[i].start()

        def peer(t):
            return (x - t + 4) % 4

        def gather_far(buf, send, recv):
            to_head(
                buf.at[x], buf.at[x], send.at[2], recv.at[2], device(0, 2, 0)
            ).start()

        def gather_near(buf, send, recv):
            for t in (1, 3):
                to_head(
                    buf.at[x], buf.at[x], send.at[t], recv.at[t], device(0, t, 0)
                ).start()

        def gather_wait(buf, recv, t):
            if t > 0:
                await_bytes(buf.at[peer(t)], recv.at[t])

        y = s % 2
        pair_seq = s + 1 - 2 * y
        pair_slot = (2 * y - 1 + n_seq) % n_seq

        def slot_rows(r):
            return pl.ds(pl.multiple_of(r * part, part), part)

        def pair_copy(buf, send, recv):
            return to_seq(
                buf.at[own_rows, :],
                buf.at[slot_rows((1 - 2 * y + n_seq) % n_seq), :],
                send, recv, pair_seq,
            )

        z_order = sorted(range(2, n_seq, 2), key=lambda r: abs(2 * r - n_seq))

        def spread_own(buf, send, recv):
            for r in z_order:
                to_seq(
                    buf.at[own_rows, :], buf.at[pl.ds(r * part, part), :],
                    send, recv, (s + r) % n_seq,
                ).start()

        def spread_pair(buf, send, recv):
            for r in z_order:
                to_seq(
                    buf.at[slot_rows(pair_slot), :],
                    buf.at[slot_rows((r + 2 * y - 1 + n_seq) % n_seq), :],
                    send, recv, (s + r) % n_seq,
                ).start()

        pair_k = pair_copy(k_all, pair_kv_send.at[0], pair_kv_recv.at[0])
        pair_v = pair_copy(v_all, pair_kv_send.at[1], pair_kv_recv.at[1])
        pair_k.start()
        pair_v.start()
        gather_near(q_all, q_send, q_recv)
        spread_own(k_all, k_send, k_recv)

        for i in range(EARLY, chips):
            product_step(i)
            oth_copies[i].start()
            pair_step(i - EARLY)
        for i in range(chips - EARLY, chips):
            pair_step(i)

        gather_far(q_all, q_send, q_recv)
        pair_k.wait_recv()
        spread_pair(k_all, k_send, k_recv)
        spread_own(v_all, v_send, v_recv)
        pair_v.wait_recv()
        spread_pair(v_all, v_send, v_recv)

        lane = lax.broadcasted_iota(jnp.int32, (1, ROWS), 1)
        q_pos = jnp.where(
            lane < ROWS // 2,
            bo[2 * s] * (ROWS // 2) + lane,
            bo[2 * s + 1] * (ROWS // 2) + lane - ROWS // 2,
        )
        start1 = dl[0]
        start2 = start1 + dl[1]
        start3 = start2 + dl[2]
        q_begin = jnp.zeros((1, ROWS), jnp.int32)
        for begin in (start1, start2, start3):
            q_begin = jnp.maximum(q_begin, jnp.where(begin <= q_pos, begin, 0))
        for side, group_index in enumerate((j, j + 1 - 2 * core)):
            for r in range(n_seq):
                slot = (s - r + n_seq) % n_seq
                base = (
                    bo[2 * slot + group_index // 4] * (ROWS // 2) + (group_index % 4) * part
                )
                k_pos = base + lax.broadcasted_iota(jnp.int32, (part, ROWS), 0)
                allowed = (k_pos <= q_pos) & (k_pos >= q_begin)
                bias[pl.ds(side * keys + r * part, part), :] = jnp.where(allowed, 0.0, NEG)

        mine_rows, other_rows = pl.ds(0, keys), pl.ds(keys, keys)

        def sib_copy(buf, i):
            return to_head(
                buf.at[mine_rows, :], buf.at[other_rows, :],
                sib_send.at[i], sib_recv.at[i], sib,
            )

        sib_k, sib_v = sib_copy(k_all, 0), sib_copy(v_all, 1)
        await_bytes(k_all.at[spread_rows, :], k_recv)
        sib_k.start()

        await_bytes(c1_rx, c1_recv)
        total = mine[chips - 1]
        for i in range(chips - 1):
            total = total + c1_rx[i].astype(F32)
        do_all[x] = total.astype(BF16)
        gather_far(do_all, do_send, do_recv)
        gather_near(do_all, do_send, do_recv)
        hg_copy = pltpu.make_async_copy(do_all.at[x], hg_out, out_sem.at[0])
        hg_copy.start()

        await_bytes(v_all.at[spread_rows, :], v_recv)
        sib_v.start()
        sib_k.wait_recv()

        order = (0, 1, 3, 2)
        for t in order:
            gather_wait(q_all, q_recv, t)
            sc = contract_last(k_all[...], q_all[peer(t)]) * scale2 + bias[...]
            top = jnp.max(sc, axis=0, keepdims=True)
            e = jnp.exp2(sc - top)
            e_all[t] = e
            st_own[pl.ds(peer(t), 1), :] = top
            st_own[pl.ds(4 + peer(t), 1), :] = jnp.sum(e, axis=0, keepdims=True)

        def group_send(own, rx, send, recv):
            for slot, t in enumerate((2, 1, 3)):
                to_head(own, rx.at[slot], send, recv, device(0, t, 0)).start()

        group_send(st_own, st_rx, st_send, st_recv)

        d_own[...] = jnp.zeros_like(d_own)
        sib_v.wait_recv()
        for t in order:
            gather_wait(do_all, do_recv, t)
            dp = contract_last(v_all[...], do_all[peer(t)])
            dp_all[t] = dp
            d_own[pl.ds(peer(t), 1), :] = jnp.sum(e_all[t] * dp, axis=0, keepdims=True)
        group_send(d_own, d_rx, d_send, d_recv)

        await_bytes(st_rx, st_recv)
        tops = [st_own[0:4, :]] + [st_rx[r, 0:4, :] for r in range(3)]
        sums = [st_own[4:8, :]] + [st_rx[r, 4:8, :] for r in range(3)]
        top = jnp.maximum(jnp.maximum(tops[0], tops[1]), jnp.maximum(tops[2], tops[3]))
        scales = [jnp.exp2(item - top) for item in tops]
        norm = sums[0] * scales[0]
        for r in range(1, 4):
            norm = norm + sums[r] * scales[r]
        scales = [item / norm for item in scales]
        fac[...] = scales[0]

        def value_grad(rows):
            total = None
            for t in order:
                p = (e_all[t, rows, :] * fac[pl.ds(peer(t), 1), :]).astype(BF16)
                term = matmul(p, do_all[peer(t)])
                total = term if total is None else total + term
            return total

        half_copies = [
            to_head(half_tx.at[i], half_rx.at[i], half_send.at[i], half_recv.at[i], sib)
            for i in range(2)
        ]
        half_tx[0] = value_grad(other_rows).astype(BF16)
        half_copies[0].start()
        acc[...] = value_grad(mine_rows)
        kt_v[...] = k_all[...].astype(F32).T.astype(BF16)
        half_copies[0].wait_recv()
        dv_tx[...] = (acc[...] + half_rx[0].astype(F32)).astype(BF16)

        def scatter(tx, rx, send, recv):
            for r in seq_order:
                rows = pl.ds(r * part, part)
                to_seq(
                    tx.at[rows, :], rx.at[rows, :], send, recv, (s - r + n_seq) % n_seq
                ).start()

        scatter(dv_tx, dv_rx, dv_send, dv_recv)

        await_bytes(d_rx, d_recv)
        row_dots = d_own[0:4, :] * scales[0]
        for r in range(3):
            row_dots = row_dots + d_rx[r, 0:4, :] * scales[r + 1]
        dsum[...] = row_dots

        def key_grad(rows):
            total = None
            for t in order:
                row = pl.ds(peer(t), 1)
                p = e_all[t, rows, :] * fac[row, :]
                ds = (p * (dp_all[t, rows, :] - dsum[row, :])).astype(BF16)
                ds_all[t, rows, :] = ds
                term = matmul(ds, q_all[peer(t)])
                total = term if total is None else total + term
            return total

        half_tx[1] = key_grad(other_rows).astype(BF16)
        half_copies[1].start()
        acc[...] = key_grad(mine_rows)
        half_copies[1].wait_recv()
        dk_tx[...] = ((acc[...] + half_rx[1].astype(F32)) * scale).astype(BF16)
        scatter(dk_tx, dk_rx, dk_send, dk_recv)

        dq_copies = []
        for t in (2, 1, 3, 0):
            query_part = matmul(kt_v[...], ds_all[t]) * scale
            if t == 0:
                dq_own[...] = query_part
            else:
                dq_tx[t - 1] = query_part.astype(BF16)
                copy = to_head(
                    dq_tx.at[t - 1], dq_rx.at[t - 1], dq_send.at[t - 1], dq_recv,
                    device(0, 4 - t, 0),
                )
                copy.start()
                dq_copies.append(copy)

        def finish(tx, rx, fin, out, recv, all_send, all_recv, own_sem):
            await_bytes(rx.at[rest, :], recv)
            summed = tx[own_rows, :].astype(F32)
            for r in range(1, n_seq):
                summed = summed + rx[pl.ds(r * part, part), :].astype(F32)
            fin[...] = summed.astype(BF16)
            place = out.at[pl.ds(row0, part), pl.ds(col0, DH)]
            for shift in head_order:
                to_head(fin, place, all_send, all_recv, device(*shift)).start()
            copy = pltpu.make_async_copy(fin, place, own_sem)
            copy.start()
            return copy

        vg_copy = finish(dv_tx, dv_rx, dv_fin, vg_out, dv_recv, av_send, av_recv, out_sem.at[1])
        kg_copy = finish(dk_tx, dk_rx, dk_fin, kg_out, dk_recv, ak_send, ak_recv, out_sem.at[2])

        await_bytes(dq_rx, dq_recv)
        query_sum = dq_own[...]
        for r in range(3):
            query_sum = query_sum + dq_rx[r].astype(F32)
        qg_v[...] = query_sum.T.astype(BF16)
        qg_copy = pltpu.make_async_copy(qg_v, qg_out, out_sem.at[3])
        qg_copy.start()

        for t in range(1, 4):
            await_bytes(q_all.at[0], q_send.at[t])
            await_bytes(do_all.at[0], do_send.at[t])
        for buf, send in ((k_all, k_send), (v_all, v_send)):
            await_bytes(buf.at[spread_rows, :], send)
        for copy in [pair_k, pair_v, sib_k, sib_v, *oth_copies, *c1_copies, *half_copies]:
            copy.wait_send()
        await_bytes(st_rx, st_send)
        await_bytes(d_rx, d_send)
        hg_copy.wait()

        for buf, send in ((dv_tx, dv_send), (dk_tx, dk_send)):
            await_bytes(buf.at[rest, :], send)
        for copy in dq_copies:
            copy.wait_send()
        spread = (n_heads - 1) * part
        for sem in (av_send, ak_send, av_recv, ak_recv):
            await_bytes(q_all.at[pl.ds(0, 3), pl.ds(0, spread // 3), :], sem)
        for copy in (qg_copy, vg_copy, kg_copy):
            copy.wait()

    return kernel


def place_results(*refs):
    sems = refs[-1]
    copies = [
        pltpu.make_async_copy(refs[i], refs[4 + i], sems.at[i]) for i in range(4)
    ]
    for copy in copies:
        copy.start()
    for copy in copies:
        copy.wait()


def local(queries, key_rows, value_rows, layer_grad, w_out, block_order, doc_lengths):
    n_seq = lax.axis_size("seq")
    part = ROWS // GROUP
    keys = n_seq * part
    depth = layer_grad.shape[1]
    chips = GROUP
    vmem = pltpu.VMEM
    dma = pltpu.SemaphoreType.DMA
    both = 2 * keys
    scratch = [
        vmem((chips, 2 * DH, depth), BF16),
        vmem((ROWS, depth), BF16),
        vmem((4, ROWS, DH), BF16),
        vmem((4, ROWS, DH), BF16),
        vmem((both, DH), BF16),
        vmem((both, DH), BF16),
        vmem((DH, both), BF16),
        vmem((both, ROWS), F32),
        pltpu.SMEM(block_order.shape, jnp.int32),
        pltpu.SMEM(doc_lengths.shape, jnp.int32),
        vmem((chips, ROWS, DH), F32),
        vmem((chips, ROWS, DH), BF16),
        vmem((chips, ROWS, DH), BF16),
        vmem((chips - 1, ROWS, DH), BF16),
        vmem((chips - 1, ROWS, DH), BF16),
        vmem((4, both, ROWS), F32),
        vmem((4, both, ROWS), F32),
        vmem((4, both, ROWS), BF16),
        vmem((8, ROWS), F32),
        vmem((3, 8, ROWS), F32),
        vmem((8, ROWS), F32),
        vmem((3, 8, ROWS), F32),
        vmem((4, ROWS), F32),
        vmem((4, ROWS), F32),
        vmem((keys, DH), F32),
        vmem((2, keys, DH), BF16),
        vmem((2, keys, DH), BF16),
        vmem((keys, DH), BF16),
        vmem((keys, DH), BF16),
        vmem((keys, DH), BF16),
        vmem((keys, DH), BF16),
        vmem((part, DH), BF16),
        vmem((part, DH), BF16),
        vmem((DH, ROWS), F32),
        vmem((3, DH, ROWS), BF16),
        vmem((3, DH, ROWS), BF16),
        vmem((ROWS, DH), BF16),
        dma((chips,)),
        dma((6,)),
        dma((4,)),
        dma((4,)),
        dma((4,)),
        dma((2,)),
        dma((2,)),
        dma((2,)),
        dma((2,)),
        dma,
        dma,
        dma,
        dma,
        dma((chips,)),
        dma((chips,)),
        dma((chips - 1,)),
        dma,
        dma((4,)),
        dma((4,)),
        dma,
        dma,
        dma,
        dma,
        dma((2,)),
        dma((2,)),
        dma((3,)),
        dma,
        dma,
        dma,
        dma,
        dma,
        dma,
        dma,
        dma,
        dma,
    ]
    anywhere = pl.BlockSpec(memory_space=pl.ANY)
    shapes = (
        jax.ShapeDtypeStruct(queries.shape, BF16),
        jax.ShapeDtypeStruct(key_rows.shape, BF16),
        jax.ShapeDtypeStruct(value_rows.shape, BF16),
        jax.ShapeDtypeStruct(queries.shape, BF16),
    )
    results = pl.pallas_call(
        make_kernel(n_seq),
        out_shape=tuple(pltpu.VMEM(shape.shape, BF16) for shape in shapes),
        in_specs=[anywhere] * 7,
        out_specs=(anywhere,) * 4,
        scratch_shapes=scratch,
        compiler_params=pltpu.CompilerParams(
            collective_id=0, has_side_effects=True, vmem_limit_bytes=58 * 1024 * 1024
        ),
    )(queries, key_rows, value_rows, layer_grad, w_out, block_order, doc_lengths)
    return pl.pallas_call(
        place_results,
        out_shape=shapes,
        in_specs=[anywhere] * 4,
        out_specs=(anywhere,) * 4,
        scratch_shapes=[dma((4,))],
        compiler_params=pltpu.CompilerParams(vmem_limit_bytes=58 * 1024 * 1024),
    )(*[pltpu.with_memory_space_constraint(part_out, pltpu.VMEM) for part_out in results])


def solution(mesh):
    return jax.shard_map(
        local,
        mesh=mesh,
        in_specs=(
            P("seq", "heads"),
            P("seq", None),
            P("seq", None),
            P("seq", "heads"),
            P(None, "heads"),
            P(),
            P(),
        ),
        out_specs=(P("seq", "heads"), P("seq", None), P("seq", None), P("seq", "heads")),
        check_vma=False,
    )
```

time: 48.9 us -> 46.7 us (0.955)
  Pallas kernels: 48.2 us -> 46 us
    pallas_call x1, Pallas kernels: 47.4 us -> 45.2 us  [local(): pl.pallas_call(make_kernel(n_seq), out_shape=tuple((pltpu.VMEM(shape.shap...]
where the time goes in v4:
time: 46.7 us; the launch traced here: 46.6 us
  Pallas kernels  46 us (99%)
  between operations  0.64 us (1%)
    pallas_call x1, Pallas kernels, local(): pl.pallas_call(make_kernel(n_seq), out_shape=tuple((pltpu.VMEM(shape.shap...  45.2 us

profile of v4, /device:TPU:1, one launch (start us, length us, event | category | flops | bytes accessed | tf_op | source)
XLA Modules:
  0.0 46.6 jit_solution(11745737214215142660)
XLA Ops:
  0.6 45.2 %shard_map.102 = (bf16[256,128]{1,0:T(8,128)(2,1)S(1)}, bf16[256,256]{1,0:T(8,128)(2,1)S(1)}, bf16[256,256]{1,0:T(8,128)(2,1)S(1)}, bf16[256,128]{1,0:T(8,128)(2,1)S(1)}) custom-call(bf16[256,128]{1,0:T(8,128)(2,1)} %q_hbm.1, bf16[256,256]{1,0:T(8,128)(2,1)} %k_hbm.1, bf16[256,256]{1,0:T(8,128)(2,1)} %v_hbm.1, bf16[256,512]{1,0:T(8,128)(2,1)} %lg_hbm.1, ...), custom_call_target="tpu_custom_call" | custom-call | tf_op jit(solution)/shard_map/pallas_call | solution.py:527
  45.9 0.8 %shard_map.103 = (bf16[256,128]{1,0:T(8,128)(2,1)}, bf16[256,256]{1,0:T(8,128)(2,1)}, bf16[256,256]{1,0:T(8,128)(2,1)}, bf16[256,128]{1,0:T(8,128)(2,1)}) custom-call(bf16[256,128]{1,0:T(8,128)(2,1)S(1)} %get-tuple-element.8.refs_0_, bf16[256,256]{1,0:T(8,128)(2,1)S(1)} %get-tuple-element.9.refs_1_, bf16[256,256]{1,0:T(8,128)(2,1)S(1)} %get-tuple-element.10.refs_2_, ...), custom_call_target="tpu_custom_call" | custom-call | tf_op jit(solution)/shard_map/pallas_call | solution.py:537

commit v5 on v4

--- a/solution.py
+++ b/solution.py
@@ -82,6 +82,16 @@
         def await_bytes(ref, sem):
             pltpu.make_async_copy(ref, ref, sem).wait()
 
+        barrier = pltpu.get_barrier_semaphore()
+        for r in seq_order:
+            pl.semaphore_signal(
+                barrier, inc=1, device_id={"seq": (s + r) % n_seq}, device_id_type=MESH
+            )
+        for r in range(1, n_heads):
+            pl.semaphore_signal(
+                barrier, inc=1, device_id={"heads": (h + r) % n_heads}, device_id_type=MESH
+            )
+
         row0 = pl.multiple_of(j * part, part)
         col0 = pl.multiple_of(c * DH, DH)
         own_rows = pl.ds(0, part)
@@ -95,16 +105,6 @@
             )
             load.start()
             w_loads.append(load)
-        barrier = pltpu.get_barrier_semaphore()
-        for r in seq_order:
-            pl.semaphore_signal(
-                barrier, inc=1, device_id={"seq": (s + r) % n_seq}, device_id_type=MESH
-            )
-        for r in range(1, n_heads):
-            pl.semaphore_signal(
-                barrier, inc=1, device_id={"heads": (h + r) % n_heads}, device_id_type=MESH
-            )
-
         small_loads = [
             pltpu.make_async_copy(q_hbm, q_all.at[x], ld_sem.at[1]),
             pltpu.make_async_copy(
@@ -312,8 +312,9 @@
         def value_grad(rows):
             total = None
             for t in order:
-                p = (e_all[t, rows, :] * fac[pl.ds(peer(t), 1), :]).astype(BF16)
-                term = matmul(p, do_all[peer(t)])
+                p = e_all[t, rows, :] * fac[pl.ds(peer(t), 1), :]
+                e_all[t, rows, :] = p
+                term = matmul(p.astype(BF16), do_all[peer(t)])
                 total = term if total is None else total + term
             return total
 
@@ -347,8 +348,7 @@
             total = None
             for t in order:
                 row = pl.ds(peer(t), 1)
-                p = e_all[t, rows, :] * fac[row, :]
-                ds = (p * (dp_all[t, rows, :] - dsum[row, :])).astype(BF16)
+                ds = (e_all[t, rows, :] * (dp_all[t, rows, :] - dsum[row, :])).astype(BF16)
                 ds_all[t, rows, :] = ds
                 term = matmul(ds, q_all[peer(t)])
                 total = term if total is None else total + term

time: 46.7 us -> 46.6 us (level)
  no operation moved by 1% of the time
where the time goes in v5:
time: 46.6 us; the launch traced here: 46.5 us
  Pallas kernels  45.9 us (98%)
  between operations  0.64 us (1%)
    pallas_call x1, Pallas kernels, local(): pl.pallas_call(make_kernel(n_seq), out_shape=tuple((pltpu.VMEM(shape.shap...  45.1 us

profile of v5, /device:TPU:1, one launch (start us, length us, event | category | flops | bytes accessed | tf_op | source)
XLA Modules:
  0.0 46.5 jit_solution(1559419804172178370)
XLA Ops:
  0.6 45.1 %shard_map.102 = (bf16[256,128]{1,0:T(8,128)(2,1)S(1)}, bf16[256,256]{1,0:T(8,128)(2,1)S(1)}, bf16[256,256]{1,0:T(8,128)(2,1)S(1)}, bf16[256,128]{1,0:T(8,128)(2,1)S(1)}) custom-call(bf16[256,128]{1,0:T(8,128)(2,1)} %q_hbm.1, bf16[256,256]{1,0:T(8,128)(2,1)} %k_hbm.1, bf16[256,256]{1,0:T(8,128)(2,1)} %v_hbm.1, bf16[256,512]{1,0:T(8,128)(2,1)} %lg_hbm.1, ...), custom_call_target="tpu_custom_call" | custom-call | tf_op jit(solution)/shard_map/pallas_call | solution.py:527
  45.8 0.8 %shard_map.103 = (bf16[256,128]{1,0:T(8,128)(2,1)}, bf16[256,256]{1,0:T(8,128)(2,1)}, bf16[256,256]{1,0:T(8,128)(2,1)}, bf16[256,128]{1,0:T(8,128)(2,1)}) custom-call(bf16[256,128]{1,0:T(8,128)(2,1)S(1)} %get-tuple-element.8.refs_0_, bf16[256,256]{1,0:T(8,128)(2,1)S(1)} %get-tuple-element.9.refs_1_, bf16[256,256]{1,0:T(8,128)(2,1)S(1)} %get-tuple-element.10.refs_2_, ...), custom_call_target="tpu_custom_call" | custom-call | tf_op jit(solution)/shard_map/pallas_call | solution.py:537

commit v6 on v5

--- a/solution.py
+++ b/solution.py
@@ -264,8 +264,8 @@
         for i in range(chips - 1):
             total = total + c1_rx[i].astype(F32)
         do_all[x] = total.astype(BF16)
+        gather_near(do_all, do_send, do_recv)
         gather_far(do_all, do_send, do_recv)
-        gather_near(do_all, do_send, do_recv)
         hg_copy = pltpu.make_async_copy(do_all.at[x], hg_out, out_sem.at[0])
         hg_copy.start()
 

time: 46.6 us -> 46 us (0.987)
  Pallas kernels: 45.9 us -> 45.2 us
    pallas_call x1, Pallas kernels: 45.1 us -> 44.5 us  [local(): pl.pallas_call(make_kernel(n_seq), out_shape=tuple((pltpu.VMEM(shape.shap...]
where the time goes in v6:
time: 46 us; the launch traced here: 45.9 us
  Pallas kernels  45.2 us (98%)
  between operations  0.64 us (1%)
    pallas_call x1, Pallas kernels, local(): pl.pallas_call(make_kernel(n_seq), out_shape=tuple((pltpu.VMEM(shape.shap...  44.5 us

profile of v6, /device:TPU:1, one launch (start us, length us, event | category | flops | bytes accessed | tf_op | source)
XLA Modules:
  0.0 45.9 jit_solution(570744895001927768)
XLA Ops:
  0.6 44.5 %shard_map.102 = (bf16[256,128]{1,0:T(8,128)(2,1)S(1)}, bf16[256,256]{1,0:T(8,128)(2,1)S(1)}, bf16[256,256]{1,0:T(8,128)(2,1)S(1)}, bf16[256,128]{1,0:T(8,128)(2,1)S(1)}) custom-call(bf16[256,128]{1,0:T(8,128)(2,1)} %q_hbm.1, bf16[256,256]{1,0:T(8,128)(2,1)} %k_hbm.1, bf16[256,256]{1,0:T(8,128)(2,1)} %v_hbm.1, bf16[256,512]{1,0:T(8,128)(2,1)} %lg_hbm.1, ...), custom_call_target="tpu_custom_call" | custom-call | tf_op jit(solution)/shard_map/pallas_call | solution.py:527
  45.1 0.8 %shard_map.103 = (bf16[256,128]{1,0:T(8,128)(2,1)}, bf16[256,256]{1,0:T(8,128)(2,1)}, bf16[256,256]{1,0:T(8,128)(2,1)}, bf16[256,128]{1,0:T(8,128)(2,1)}) custom-call(bf16[256,128]{1,0:T(8,128)(2,1)S(1)} %get-tuple-element.8.refs_0_, bf16[256,256]{1,0:T(8,128)(2,1)S(1)} %get-tuple-element.9.refs_1_, bf16[256,256]{1,0:T(8,128)(2,1)S(1)} %get-tuple-element.10.refs_2_, ...), custom_call_target="tpu_custom_call" | custom-call | tf_op jit(solution)/shard_map/pallas_call | solution.py:537

commit v7 on v6

--- a/solution.py
+++ b/solution.py
@@ -284,7 +284,7 @@
             st_own[pl.ds(4 + peer(t), 1), :] = jnp.sum(e, axis=0, keepdims=True)
 
         def group_send(own, rx, send, recv):
-            for slot, t in enumerate((2, 1, 3)):
+            for slot, t in enumerate((1, 3, 2)):
                 to_head(own, rx.at[slot], send, recv, device(0, t, 0)).start()
 
         group_send(st_own, st_rx, st_send, st_recv)

time: 46 us -> 45.9 us (level)
  no operation moved by 1% of the time
where the time goes in v7:
time: 45.9 us; the launch traced here: 45.8 us
  Pallas kernels  45.1 us (98%)
  between operations  0.64 us (1%)
    pallas_call x1, Pallas kernels, local(): pl.pallas_call(make_kernel(n_seq), out_shape=tuple((pltpu.VMEM(shape.shap...  44.4 us

profile of v7, /device:TPU:1, one launch (start us, length us, event | category | flops | bytes accessed | tf_op | source)
XLA Modules:
  0.0 45.8 jit_solution(776984558795419556)
XLA Ops:
  0.6 44.4 %shard_map.102 = (bf16[256,128]{1,0:T(8,128)(2,1)S(1)}, bf16[256,256]{1,0:T(8,128)(2,1)S(1)}, bf16[256,256]{1,0:T(8,128)(2,1)S(1)}, bf16[256,128]{1,0:T(8,128)(2,1)S(1)}) custom-call(bf16[256,128]{1,0:T(8,128)(2,1)} %q_hbm.1, bf16[256,256]{1,0:T(8,128)(2,1)} %k_hbm.1, bf16[256,256]{1,0:T(8,128)(2,1)} %v_hbm.1, bf16[256,512]{1,0:T(8,128)(2,1)} %lg_hbm.1, ...), custom_call_target="tpu_custom_call" | custom-call | tf_op jit(solution)/shard_map/pallas_call | solution.py:527
  45.0 0.8 %shard_map.103 = (bf16[256,128]{1,0:T(8,128)(2,1)}, bf16[256,256]{1,0:T(8,128)(2,1)}, bf16[256,256]{1,0:T(8,128)(2,1)}, bf16[256,128]{1,0:T(8,128)(2,1)}) custom-call(bf16[256,128]{1,0:T(8,128)(2,1)S(1)} %get-tuple-element.8.refs_0_, bf16[256,256]{1,0:T(8,128)(2,1)S(1)} %get-tuple-element.9.refs_1_, bf16[256,256]{1,0:T(8,128)(2,1)S(1)} %get-tuple-element.10.refs_2_, ...), custom_call_target="tpu_custom_call" | custom-call | tf_op jit(solution)/shard_map/pallas_call | solution.py:537
